TPU v7x, 256 devices: a whole 4x4x8 slice. The times are simulated.
256 devices in a mesh: row: 16 (over x, z_hi, core), col: 16 (over y, z_lo).
Axes of the slice: x: 4, y: 4, z: 8 (z_hi: 2, z_lo: 4; z = z_hi * 4 + z_lo), core: 2. Of those that a mesh axis runs over, the one named last changes fastest.
Arguments:
- tokens: bfloat16 [768, 6144], P('col', 'row'), may hold values from -6 to 6
- gate_weight: bfloat16 [6144, 14336], P('row', 'col'), may hold values from -0.078125 to 0.078125
- up_weight: bfloat16 [6144, 14336], P('row', 'col'), may hold values from -0.078125 to 0.078125
- down_weight: bfloat16 [14336, 6144], P('col', 'row'), may hold values from -0.046875 to 0.046875
- cotangent: bfloat16 [768, 6144], P('col', 'row'), may hold values from -6 to 6
Outputs:
- output: bfloat16 [768, 6144], P('col', 'row')
- grad_input: bfloat16 [768, 6144], P('col', 'row')
- grad_gate: float32 [6144, 14336], P('row', 'col')
- grad_up: float32 [6144, 14336], P('row', 'col')
- grad_down: float32 [14336, 6144], P('col', 'row')
All inputs are finite; a program needn't handle non-finite values.
Results may differ from a plain program's by a relative error of at most 0.0049.
Values may be sent and summed in bfloat16 or wider, within the bound.
A program may use at most 64 MiB of HBM per device.

v0:
```python
import jax
import jax.numpy as jnp
from jax import lax
from jax.sharding import PartitionSpec as P


def contract_first(left, right):
    return lax.dot_general(
        left, right, (((0,), (0,)), ((), ())), preferred_element_type=jnp.float32
    )


def contract_last(left, right):
    return lax.dot_general(
        left, right, (((1,), (1,)), ((), ())), preferred_element_type=jnp.float32
    )


def body(tokens, gate_weight, up_weight, down_weight, cotangent):
    total_tokens = tokens.shape[0] * lax.axis_size("col")
    scale = total_tokens ** (-0.5)
    own_rows = tokens.shape[0]

    def token_panel(piece):
        return lax.all_gather(piece, "col", axis=0, tiled=True)

    def share_total(stacked):
        return lax.psum_scatter(stacked, "row", scatter_dimension=1, tiled=True)

    def share_gather(stacked):
        return lax.all_gather(stacked, "row", axis=1, tiled=True)

    def owner_total(term):
        return lax.psum_scatter(
            term(jnp.int32(0), own_rows * lax.axis_size("col")),
            "col",
            scatter_dimension=0,
            tiled=True,
        )

    token_all = token_panel(tokens)
    gate_part = jnp.dot(token_all, gate_weight, preferred_element_type=jnp.float32)
    up_part = jnp.dot(token_all, up_weight, preferred_element_type=jnp.float32)
    stacked = jnp.stack([gate_part, up_part])
    summed = share_total(stacked)
    gate = summed[0]
    up = summed[1]
    sig = jax.nn.sigmoid(gate)
    hidden = (gate * sig * up).astype(jnp.bfloat16)
    hidden_all = share_gather(hidden[None])[0]

    def forward_term(start, count):
        return jnp.dot(hidden_all, down_weight, preferred_element_type=jnp.float32)

    output = owner_total(forward_term).astype(jnp.bfloat16)
    cot_all = token_panel(cotangent)
    grad_down = contract_first(hidden_all, cot_all) * scale
    hidden_part = contract_last(cot_all, down_weight)
    d_hidden = share_total(hidden_part[None])[0]
    d_up = (d_hidden * gate * sig).astype(jnp.bfloat16)
    d_gate = (d_hidden * up * sig * (1.0 + gate * (1.0 - sig))).astype(jnp.bfloat16)
    grads_local = jnp.stack([d_gate, d_up])
    grads_all = share_gather(grads_local)
    grad_gate = contract_first(token_all, grads_all[0]) * scale
    grad_up = contract_first(token_all, grads_all[1]) * scale

    def backward_term(start, count):
        return contract_last(grads_all[0], gate_weight) + contract_last(grads_all[1], up_weight)

    grad_input = owner_total(backward_term).astype(jnp.bfloat16)
    return (output, grad_input, grad_gate, grad_up, grad_down)


def solution(mesh):
    return jax.shard_map(
        body,
        mesh=mesh,
        in_specs=(
            P("col", "row"),
            P("row", "col"),
            P("row", "col"),
            P("col", "row"),
            P("col", "row"),
        ),
        out_specs=(
            P("col", "row"),
            P("col", "row"),
            P("row", "col"),
            P("row", "col"),
            P("col", "row"),
        ),
        check_vma=False,
    )
```

profile of v0, /device:TPU:1, one launch (start us, length us, event | category | flops | bytes accessed | tf_op | source)
XLA Modules:
  0.0 559.7 jit_solution(9468772664622326178)
XLA Ops:
  7.2 0.0 reduce-scatter.9.cloned.1.call-start
  7.2 43.1 %all_gather.14 = bf16[768,384]{1,0:T(8,128)(2,1)S(1)} all-gather(bf16[48,384]{1,0:T(8,128)(2,1)} %param.9), channel_id=1, replica_groups=mesh['row'=16,'col'=16] {'col'}, dimensions={0}, use_global_device_ids=true | all-gather | bytes 626688 | tf_op jit(solution)/shard_map/all_gather | solution.py:25
  50.3 2.5 convolution_bitcast_fusion
  52.8 0.0 reduce-scatter.5.cloned.1.call-start
  52.8 0.7 copy-done.4
  53.5 36.6 %all_gather.12 = bf16[768,384]{1,0:T(8,128)(2,1)S(1)} all-gather(bf16[48,384]{1,0:T(8,128)(2,1)S(1)} %copy-done.4), channel_id=1, replica_groups=mesh['row'=16,'col'=16] {'col'}, dimensions={0}, use_global_device_ids=true | all-gather | bytes 626688 | tf_op jit(solution)/shard_map/all_gather | solution.py:25
  90.1 0.9 convolution_bitcast_fusion.1
  91.1 0.2 copy-done.3
  91.2 0.9 convolution_bitcast_fusion.2
  92.2 2.8 pad_maximum_fusion
  95.0 0.0 all-gather.3.cloned.1.call-start
  95.0 54.7 %reduce-scatter.9.cloned.1.call-done = f32[1,48,896]{2,1,0:T(8,128)} async-done(((f32[1,768,896]{2,1,0:T(8,128)}), f32[1,48,896]{2,1,0:T(8,128)}) %reduce-scatter.9.cloned.1.call-update) | async-done | bytes 172048 | tf_op jit(solution)/shard_map/reduce_scatter | solution.py:28
  149.7 114.8 %reduce-scatter.5.cloned.1.call-done = f32[2,48,896]{2,1,0:T(8,128)} async-done(((f32[2,768,896]{2,1,0:T(8,128)}), f32[2,48,896]{2,1,0:T(8,128)}) %reduce-scatter.5.cloned.1.call-update) | async-done | bytes 344080 | tf_op jit(solution)/shard_map/reduce_scatter | solution.py:28
  264.5 1.8 multiply_convert_fusion.1
  266.3 0.0 all-gather.5.cloned.1.call-start
  266.4 0.7 pad_maximum_fusion.1
  267.1 0.0 reduce-scatter.7.cloned.1.call-start
  267.2 56.7 %all-gather.3.cloned.1.call-done = bf16[1,768,896]{2,1,0:T(8,128)(2,1)} async-done(((bf16[1,48,896]{2,1,0:T(8,128)(2,1)}), bf16[1,768,896]{2,1,0:T(8,128)(2,1)}) %all-gather.3.cloned.1.call-update) | async-done | bytes 1376272 | tf_op jit(solution)/shard_map/all_gather | solution.py:31
  323.8 3.3 fusion.3
  327.1 0.0 reduce-scatter.11.cloned.1.call-start
  327.1 63.6 %all-gather.5.cloned.1.call-done = bf16[2,768,896]{2,1,0:T(8,128)(2,1)} async-done(((bf16[2,48,896]{2,1,0:T(8,128)(2,1)}), bf16[2,768,896]{2,1,0:T(8,128)(2,1)}) %all-gather.5.cloned.1.call-update) | async-done | bytes 2752528 | tf_op jit(solution)/shard_map/all_gather | solution.py:31
  390.8 2.4 fusion.5
  393.2 2.0 convolution_add_fusion
  395.2 3.3 convolution_multiply_fusion
  398.5 67.1 %reduce-scatter.7.cloned.1.call-done = f32[48,384]{1,0:T(8,128)} async-done(((f32[768,384]{1,0:T(8,128)}), f32[48,384]{1,0:T(8,128)}) %reduce-scatter.7.cloned.1.call-update) | async-done | bytes 73744 | tf_op jit(solution)/shard_map/reduce_scatter | solution.py:34
  465.6 1.5 convert_element_type.19
  467.1 2.2 fusion.1
  469.4 1.5 copy.10
  470.9 2.2 fusion
  473.1 1.5 copy.11
  474.6 76.7 %reduce-scatter.11.cloned.1.call-done = f32[48,384]{1,0:T(8,128)} async-done(((f32[768,384]{1,0:T(8,128)}), f32[48,384]{1,0:T(8,128)}) %reduce-scatter.11.cloned.1.call-update) | async-done | bytes 73744 | tf_op jit(solution)/shard_map/reduce_scatter | solution.py:34
  551.4 1.5 convert_element_type.22
  (14 shorter events, 0.1 us)
Async XLA Ops:
  7.2 43.1 %copy-start = (bf16[896,384]{1,0:T(8,128)(2,1)S(1)}, bf16[896,384]{1,0:T(8,128)(2,1)}, u32[]{:S(2)}) copy-start(bf16[896,384]{1,0:T(8,128)(2,1)} %param.8) | copy-start | bytes 2064388
  7.2 142.5 %reduce-scatter.9.cloned.1.call-start = ((), (), s32[]{:S(2)}) async-start(), calls=%async_computation.7 | async-start | bytes 2924544 | tf_op jit(solution)/shard_map/reduce_scatter | solution.py:28
  52.8 0.8 copy-start.4
  52.8 37.4 %copy-start.1 = (bf16[384,896]{1,0:T(8,128)(2,1)S(1)}, bf16[384,896]{1,0:T(8,128)(2,1)}, u32[]{:S(2)}) copy-start(bf16[384,896]{1,0:T(8,128)(2,1)} %param.7) | copy-start | bytes 2064388
  52.8 211.7 %reduce-scatter.5.cloned.1.call-start = ((), (), s32[]{:S(2)}) async-start(), calls=%async_computation.4 | async-start | bytes 5849088 | tf_op jit(solution)/shard_map/reduce_scatter | solution.py:28
  90.1 1.1 copy-start.3
  95.0 228.9 %all-gather.3.cloned.1.call-start = ((), (), s32[]{:S(2)}) async-start(), calls=%async_computation.5 | async-start | bytes 1462272 | tf_op jit(solution)/shard_map/all_gather | solution.py:31
  266.3 124.4 %all-gather.5.cloned.1.call-start = ((), (), s32[]{:S(2)}) async-start(), calls=%async_computation.8 | async-start | bytes 2924544 | tf_op jit(solution)/shard_map/all_gather | solution.py:31
  267.1 198.5 %reduce-scatter.7.cloned.1.call-start = ((), (), s32[]{:S(2)}) async-start(), calls=%async_computation.6 | async-start | bytes 1253376 | tf_op jit(solution)/shard_map/reduce_scatter | solution.py:34
  327.1 224.3 %reduce-scatter.11.cloned.1.call-start = ((), (), s32[]{:S(2)}) async-start(), calls=%async_computation.9 | async-start | bytes 1253376 | tf_op jit(solution)/shard_map/reduce_scatter | solution.py:34
  390.8 2.4 copy-start.2
Sparse Core Ops, SparseCore 0:
  52.9 96.7 reduce-scatter.8
  154.0 110.4 reduce-scatter.4
  268.0 55.7 all-gather.2
  327.3 63.4 all-gather.4
  393.9 71.7 reduce-scatter.6
  468.2 83.1 reduce-scatter.10
where the time goes:
time: 571 us; the launch traced here: 560 us
  waiting for transfers between devices  434 us (76%)
  blocking collectives  79.7 us (14%)
  matrix products  19.8 us (3%)
  between operations  14.2 us (2%)
  other arithmetic  8.28 us (1%)
    reduce_scatter x2, waiting for transfers between devices, share_total(): return lax.psum_scatter(stacked, 'row', scatter_dimension=1, tiled=True)  169 us
    reduce_scatter x2, waiting for transfers between devices, owner_total(): lax.psum_scatter(term(jnp.int32(0), own_rows * lax.axis_size('col')), 'co...  144 us
    all_gather x2, waiting for transfers between devices, share_gather(): return lax.all_gather(stacked, 'row', axis=1, tiled=True)  120 us
    all_gather x2, blocking collectives, token_panel(): return lax.all_gather(piece, 'col', axis=0, tiled=True)  79.7 us
  transfers between devices with their start and end apart: 6, of which 6 were waited for; matrix products, arithmetic and copies ran while one was open for 5% of the time, Pallas kernels for 0%

commit v1 on v0

v1 whole, which is shorter than its diff:
```python
import functools

import jax
import jax.numpy as jnp
from jax import lax
from jax.experimental import pallas as pl
from jax.experimental.pallas import tpu as pltpu
from jax.sharding import PartitionSpec as P

STAGES = 3
BF16 = jnp.bfloat16
F32 = jnp.float32


def dot(a, b, dims):
    return lax.dot_general(a, b, (dims, ((), ())), preferred_element_type=F32)


def kernel(
    scale,
    tok_in, wg_in, wu_in, wd_in, cot_in,
    out_ref, gin_ref, gg_hbm, gu_hbm, gd_hbm,
    panel, other, wg, wu, wd,
    part, part_own, rs_x, zs, zr, hid,
    oparts, oparts_own, rs_y, zout, rs_z,
    gg, gu, gd,
    load_sem, wsend, wrecv,
    azs, azr, ays, ayr, afs, afr,
    xrs, xrr, z4s, z4r, xas, xar, hfs, hfr,
    yrs, yrr, zrs, zrr, store_sem,
):
    row = lax.axis_index("row")
    col = lax.axis_index("col")
    x = row // 4
    zh = (row // 2) % 2
    k = row % 2
    y = col // 4
    zl = col % 4

    def at(dx=0, dz4=0, dk=0, dy=0, dz=0):
        xx = (x + dx) % 4
        zz = (zh + dz4) % 2
        kk = (k + dk) % 2
        yy = (y + dy) % 4
        ll = (zl + dz) % 4
        return {"row": xx * 4 + zz * 2 + kk, "col": yy * 4 + ll}

    sends = []

    def remote(src, dst, ssem, rsem, device):
        copy = pltpu.make_async_remote_copy(
            src_ref=src, dst_ref=dst, send_sem=ssem, recv_sem=rsem,
            device_id=device, device_id_type=pl.DeviceIdType.MESH,
        )
        copy.start()
        sends.append(copy)
        return copy

    loads = []
    ins = (tok_in, cot_in)
    for tc in range(2):
        for j in range(STAGES):
            loads.append(pltpu.make_async_copy(
                ins[tc].at[pl.ds(16 * j, 16)],
                panel.at[j, tc, zl // 2, y, zl % 2],
                load_sem.at[tc * STAGES + j],
            ))
    for i, (src, dst) in enumerate(((wg_in, wg), (wu_in, wu), (wd_in, wd))):
        loads.append(pltpu.make_async_copy(src, dst.at[0], load_sem.at[2 * STAGES + i]))
    for load in loads:
        load.start()

    barrier = pltpu.get_barrier_semaphore()
    peers = [at(dk=1), at(dz4=1)]
    peers += [at(dx=d) for d in (1, 2, 3)]
    peers += [at(dy=d) for d in (1, 2, 3)]
    peers += [at(dz=d) for d in (1, 2, 3)]
    for peer in peers:
        pl.semaphore_signal(barrier, inc=1, device_id=peer, device_id_type=pl.DeviceIdType.MESH)
    pl.semaphore_wait(barrier, len(peers))

    az = {}
    for j in range(STAGES):
        for tc in range(2):
            for d in (1, 2, 3):
                az[j, tc, d] = remote(
                    ins[tc].at[pl.ds(16 * j, 16)],
                    panel.at[j, tc, zl // 2, y, zl % 2],
                    azs.at[j, tc, d - 1], azr.at[j, tc, d - 1], at(dz=d),
                )
    wx = []
    for i, (src, dst) in enumerate(((wg_in, wg), (wu_in, wu), (wd_in, wd))):
        wx.append(remote(src, dst.at[1], wsend.at[i], wrecv.at[i], at(dk=1)))

    ay, af = {}, {}

    def gather_y(j):
        for tc in range(2):
            loads[tc * STAGES + j].wait()
            for d in (1, 2, 3):
                az[j, tc, d].wait_recv()
            for d in (1, 2, 3):
                ay[j, tc, d] = remote(
                    panel.at[j, tc, :, y], panel.at[j, tc, :, y],
                    ays.at[j, tc, d - 1], ayr.at[j, tc, d - 1], at(dy=d),
                )

    def forward_core(j):
        for tc in range(2):
            for d in (1, 2, 3):
                ay[j, tc, d].wait_recv()
            af[j, tc] = remote(
                panel.at[j, tc, 1 - k], other.at[j, tc],
                afs.at[j, tc], afr.at[j, tc], at(dk=1),
            )

    xr = {}

    def partials(j):
        for a in range(3):
            tc = 0 if a < 2 else 1
            if a != 1:
                af[j, tc].wait_recv()
            if j == 0:
                loads[2 * STAGES + a].wait()
                wx[a].wait_recv()
            lhs0 = panel[j, tc, k].reshape(128, 384)
            lhs1 = other[j, tc].reshape(128, 384)
            w = (wg, wu, wd)[a]
            if a < 2:
                res = dot(lhs0, w[0], ((1,), (0,))) + dot(lhs1, w[1], ((1,), (0,)))
            else:
                res = dot(lhs0, w[0], ((1,), (1,))) + dot(lhs1, w[1], ((1,), (1,)))
            part_own[j, a] = res.reshape(4, 32, 896)
            part[j, a] = res.astype(BF16).reshape(4, 32, 896)
            for d in (2, 1, 3):
                xr[j, a, d] = remote(
                    part.at[j, a, (x + d) % 4], rs_x.at[j, a, d - 1],
                    xrs.at[j, a, d - 1], xrr.at[j, a, d - 1], at(dx=d),
                )

    z4 = {}

    def sum_x(j):
        for a in range(3):
            for d in (1, 2, 3):
                xr[j, a, d].wait_recv()
            total = part_own[j, a, x]
            for d in (1, 2, 3):
                total = total + rs_x[j, a, d - 1].astype(F32)
            part_own[j, a, x] = total
            zs[j, a] = total.astype(BF16)
            z4[j, a] = remote(
                zs.at[j, a], zr.at[j, a], z4s.at[j, a], z4r.at[j, a], at(dz4=1),
            )

    xa, hf = {}, {}

    def spread(j, a, value):
        hid[j, a, k, x] = value.astype(BF16)
        for d in (2, 1, 3):
            xa[j, a, d] = remote(
                hid.at[j, a, k, x], hid.at[j, a, k, x],
                xas.at[j, a, d - 1], xar.at[j, a, d - 1], at(dx=d),
            )

    def middle(j):
        z4[j, 0].wait_recv()
        z4[j, 1].wait_recv()
        gate = part_own[j, 0, x] + zr[j, 0].astype(F32)
        up = part_own[j, 1, x] + zr[j, 1].astype(F32)
        sig = jax.nn.sigmoid(gate)
        spread(j, 0, gate * sig * up)
        z4[j, 2].wait_recv()
        d_hidden = part_own[j, 2, x] + zr[j, 2].astype(F32)
        spread(j, 1, d_hidden * up * sig * (1.0 + gate * (1.0 - sig)))
        spread(j, 2, d_hidden * gate * sig)

    def forward_hidden(j):
        for a in range(3):
            for d in (1, 2, 3):
                xa[j, a, d].wait_recv()
            hf[j, a] = remote(
                hid.at[j, a, k], hid.at[j, a, k], hfs.at[j, a], hfr.at[j, a], at(dk=1),
            )

    yr = {}

    def send_y(j, b, res):
        res = res.reshape(2, 4, 32, 384)
        oparts_own[j, b] = res
        oparts[j, b] = res.astype(BF16)
        for d in (2, 1, 3):
            yr[j, b, d] = remote(
                oparts.at[j, b, :, (y + d) % 4], rs_y.at[j, b, d - 1],
                yrs.at[j, b, d - 1], yrr.at[j, b, d - 1], at(dy=d),
            )

    def back(j):
        for a in range(3):
            hf[j, a].wait_recv()
        h = hid[j, 0].reshape(256, 896)
        dg = hid[j, 1].reshape(256, 896)
        du = hid[j, 2].reshape(256, 896)
        send_y(j, 0, dot(h, wd[0], ((1,), (0,))))
        send_y(j, 1, dot(dg, wg[0], ((1,), (1,))) + dot(du, wu[0], ((1,), (1,))))

    def grads(j):
        h = hid[j, 0].reshape(256, 896)
        dg = hid[j, 1].reshape(256, 896)
        du = hid[j, 2].reshape(256, 896)
        tok = panel[j, 0].reshape(256, 384)
        cot = panel[j, 1].reshape(256, 384)
        for acc, l, r in ((gg, tok, dg), (gu, tok, du), (gd, h, cot)):
            term = dot(l, r, ((0,), (0,)))
            if j > 0:
                term = acc[...] + term
            if j == STAGES - 1:
                term = term * scale
            acc[...] = term

    zrc = {}

    def sum_y(j):
        for b in range(2):
            for d in (1, 2, 3):
                yr[j, b, d].wait_recv()
            total = oparts_own[j, b, :, y]
            for d in (1, 2, 3):
                total = total + rs_y[j, b, d - 1].astype(F32)
            oparts_own[j, b, :, y] = total
            zout[j, b] = total.astype(zout.dtype).reshape(4, 16, 384)
            for d in (1, 2, 3):
                zrc[j, b, d] = remote(
                    zout.at[j, b, (zl + d) % 4], rs_z.at[j, b, d - 1],
                    zrs.at[j, b, d - 1], zrr.at[j, b, d - 1], at(dz=d),
                )

    def finish(j):
        for b in range(2):
            for d in (1, 2, 3):
                zrc[j, b, d].wait_recv()
            total = oparts_own[j, b, zl // 2, y, pl.ds(pl.multiple_of(zl % 2 * 16, 16), 16)]
            for d in (1, 2, 3):
                total = total + rs_z[j, b, d - 1].astype(F32)
            (out_ref, gin_ref)[b][pl.ds(16 * j, 16)] = total.astype(BF16)

    gather_y(0)
    gather_y(1)
    forward_core(0)
    gather_y(2)
    partials(0)
    forward_core(1)
    partials(1)
    forward_core(2)
    partials(2)
    sum_x(0)
    sum_x(1)
    middle(0)
    sum_x(2)
    middle(1)
    forward_hidden(0)
    middle(2)
    back(0)
    grads(0)
    forward_hidden(1)
    back(1)
    grads(1)
    sum_y(0)
    forward_hidden(2)
    back(2)
    sum_y(1)
    finish(0)
    grads(2)
    stores = []
    for i, (src, dst) in enumerate(((gg, gg_hbm), (gu, gu_hbm), (gd, gd_hbm))):
        store = pltpu.make_async_copy(src, dst, store_sem.at[i])
        store.start()
        stores.append(store)
    sum_y(2)
    finish(1)
    finish(2)
    for store in stores:
        store.wait()
    for copy in sends:
        copy.wait_send()


def body(tokens, gate_weight, up_weight, down_weight, cotangent):
    total_tokens = tokens.shape[0] * lax.axis_size("col")
    scale = total_tokens ** (-0.5)
    vmem = pl.BlockSpec(memory_space=pltpu.VMEM)
    hbm = pl.BlockSpec(memory_space=pl.ANY)
    S = STAGES
    sem = pltpu.SemaphoreType.DMA
    scratch = [
        pltpu.VMEM((S, 2, 2, 4, 2, 16, 384), BF16),
        pltpu.VMEM((S, 2, 4, 2, 16, 384), BF16),
        pltpu.VMEM((2, 384, 896), BF16),
        pltpu.VMEM((2, 384, 896), BF16),
        pltpu.VMEM((2, 896, 384), BF16),
        pltpu.VMEM((S, 3, 4, 32, 896), BF16),
        pltpu.VMEM((S, 3, 4, 32, 896), F32),
        pltpu.VMEM((S, 3, 3, 32, 896), BF16),
        pltpu.VMEM((S, 3, 32, 896), BF16),
        pltpu.VMEM((S, 3, 32, 896), BF16),
        pltpu.VMEM((S, 3, 2, 4, 32, 896), BF16),
        pltpu.VMEM((S, 2, 2, 4, 32, 384), BF16),
        pltpu.VMEM((S, 2, 2, 4, 32, 384), F32),
        pltpu.VMEM((S, 2, 3, 2, 32, 384), BF16),
        pltpu.VMEM((S, 2, 4, 16, 384), BF16),
        pltpu.VMEM((S, 2, 3, 16, 384), BF16),
        pltpu.VMEM((384, 896), F32),
        pltpu.VMEM((384, 896), F32),
        pltpu.VMEM((896, 384), F32),
        sem((2 * S + 3,)), sem((3,)), sem((3,)),
        sem((S, 2, 3)), sem((S, 2, 3)), sem((S, 2, 3)), sem((S, 2, 3)), sem((S, 2)), sem((S, 2)),
        sem((S, 3, 3)), sem((S, 3, 3)), sem((S, 3)), sem((S, 3)),
        sem((S, 3, 3)), sem((S, 3, 3)), sem((S, 3)), sem((S, 3)),
        sem((S, 2, 3)), sem((S, 2, 3)), sem((S, 2, 3)), sem((S, 2, 3)), sem((3,)),
    ]
    return pl.pallas_call(
        functools.partial(kernel, scale),
        out_shape=(
            jax.ShapeDtypeStruct((48, 384), BF16),
            jax.ShapeDtypeStruct((48, 384), BF16),
            jax.ShapeDtypeStruct((384, 896), F32),
            jax.ShapeDtypeStruct((384, 896), F32),
            jax.ShapeDtypeStruct((896, 384), F32),
        ),
        in_specs=[hbm] * 5,
        out_specs=(vmem, vmem, hbm, hbm, hbm),
        scratch_shapes=scratch,
        compiler_params=pltpu.CompilerParams(
            collective_id=0, has_side_effects=True, vmem_limit_bytes=56 * 1024 * 1024,
        ),
        cost_estimate=pl.CostEstimate(
            flops=2 * 9 * 768 * 384 * 896, bytes_accessed=8 * 1024 * 1024, transcendentals=0,
        ),
        name="ffn",
    )(tokens, gate_weight, up_weight, down_weight, cotangent)


def solution(mesh):
    return jax.shard_map(
        body,
        mesh=mesh,
        in_specs=(
            P("col", "row"),
            P("row", "col"),
            P("row", "col"),
            P("col", "row"),
            P("col", "row"),
        ),
        out_specs=(
            P("col", "row"),
            P("col", "row"),
            P("row", "col"),
            P("row", "col"),
            P("col", "row"),
        ),
        check_vma=False,
    )
```

time: 571 us -> 92.2 us (0.16); the launches traced: 560 us -> 91.9 us
  waiting for transfers between devices: 434 us -> 0 us
  Pallas kernels: 0 us -> 83 us
  blocking collectives: 79.7 us -> 0 us
  matrix products: 19.8 us -> 0 us
  between operations: 14.2 us -> 0.64 us
  other arithmetic: 8.28 us -> 0 us
    reduce_scatter x4 -> x0, waiting for transfers between devices: 313 us -> none  [the longest x2 169 us: share_total(): return lax.psum_scatter(stacked, 'row', scatter_dimension=1, tiled=True)]
    all_gather x2 -> x0, waiting for transfers between devices: 120 us -> none  [share_gather(): return lax.all_gather(stacked, 'row', axis=1, tiled=True)]
    pallas_call x0 -> x1, Pallas kernels: none -> 83 us  [body(): pl.pallas_call(functools.partial(kernel, scale), out_shape=(jax.ShapeDtyp...]
    all_gather x2 -> x0, blocking collectives: 79.7 us -> none  [token_panel(): return lax.all_gather(piece, 'col', axis=0, tiled=True)]
    dot_general x9 -> x0, matrix products: 19.8 us -> none  [the longest x3 7.8 us: contract_first(): lax.dot_general(left, right, (((0,), (0,)), ((), ())), preferred_element_...]
  transfers between devices with their start and end apart: 6 -> 0, of which waited for: 6 -> 0; matrix products, arithmetic and copies ran while one was open for 5% -> 0% of each run, Pallas kernels for 0% -> 0%
where the time goes in v1:
time: 92.2 us; the launch traced here: 91.9 us
  Pallas kernels  83 us (90%)
  local copies, waits for them, and re-layouts  8.3 us (9%)
    pallas_call x1, Pallas kernels, body(): pl.pallas_call(functools.partial(kernel, scale), out_shape=(jax.ShapeDtyp...  83 us
    unnamed x9, local copies, waits for them, and re-layouts  8.3 us

profile of v1, /device:TPU:1, one launch (start us, length us, event | category | flops | bytes accessed | tf_op | source)
XLA Modules:
  0.0 91.9 jit_solution(7082858989919312218)
XLA Ops:
  0.6 83.0 %ffn.1 = (bf16[48,384]{1,0:T(8,128)(2,1)}, bf16[48,384]{1,0:T(8,128)(2,1)}, f32[384,896]{1,0:T(8,128)}, f32[384,896]{1,0:T(8,128)}, f32[896,384]{1,0:T(8,128)}) custom-call(bf16[48,384]{1,0:T(8,128)(2,1)} %tok_in.1, bf16[384,896]{1,0:T(8,128)(2,1)} %wg_in.1, bf16[384,896]{1,0:T(8,128)(2,1)} %wu_in.1, bf16[896,384]{1,0:T(8,128)(2,1)} %wd_in.1, ...), custom_call_target="tpu_custom_call" | custom-call | flops 4756340736 | bytes 8388608 | tf_op jit(solution)/shard_map/ffn/pallas_call | solution.py:322
  83.6 1.4 %copy.15 = bf16[48,384]{1,0:T(8,128)(2,1)} copy(bf16[48,384]{1,0:T(8,128)(2,1)} %get-tuple-element.10) | data formatting | bytes 73728
  85.0 1.4 %copy.16 = bf16[48,384]{1,0:T(8,128)(2,1)} copy(bf16[48,384]{1,0:T(8,128)(2,1)} %get-tuple-element.11) | data formatting | bytes 73728
  86.4 0.0 copy-start.1
  86.4 2.6 %copy.17 = f32[384,896]{1,0:T(8,128)} copy(f32[384,896]{1,0:T(8,128)} %get-tuple-element.12) | data formatting | bytes 2752512
  89.0 0.0 copy-done.1
  89.0 0.0 copy-start
  89.0 1.1 %copy.18 = f32[384,896]{1,0:T(8,128)} copy(f32[384,896]{1,0:T(8,128)S(1)} %copy-done.1) | data formatting | bytes 2752512
  90.1 0.8 copy-done
  90.9 1.1 %copy.19 = f32[896,384]{1,0:T(8,128)} copy(f32[896,384]{1,0:T(8,128)S(1)} %copy-done) | data formatting | bytes 2752512
Async XLA Ops:
  86.4 2.6 %copy-start.1 = (f32[384,896]{1,0:T(8,128)S(1)}, f32[384,896]{1,0:T(8,128)}, u32[]{:S(2)}) copy-start(f32[384,896]{1,0:T(8,128)} %get-tuple-element.13) | copy-start | bytes 4128772
  89.0 1.8 %copy-start = (f32[896,384]{1,0:T(8,128)S(1)}, f32[896,384]{1,0:T(8,128)}, u32[]{:S(2)}) copy-start(f32[896,384]{1,0:T(8,128)} %get-tuple-element.14) | copy-start | bytes 4128772

commit v2 on v0

v2 whole, which is shorter than its diff:
```python
import functools

import jax
import jax.numpy as jnp
from jax import lax
from jax.experimental import pallas as pl
from jax.experimental.pallas import tpu as pltpu
from jax.sharding import PartitionSpec as P

STAGES = 3
BF16 = jnp.bfloat16
F32 = jnp.float32


def dot(a, b, dims):
    return lax.dot_general(a, b, (dims, ((), ())), preferred_element_type=F32)


def kernel(
    scale,
    tok_in, wg_in, wu_in, wd_in, cot_in,
    out_any, gin_any, gg_any, gu_any, gd_any,
    panel, other, wg, wu, wd,
    part, part_own, rs_x, zs, zr, hid,
    oparts, oparts_own, rs_y, zout, rs_z,
    out_ref, gin_ref, big, gd,
    load_sem, wsend, wrecv,
    azs, azr, azr0, ats, atr, ays, ayr, afs, afr,
    xrs, xrr, z4s, z4r, xas, xar, xbr, hfs, hfr,
    yrs, yrr, zrs, zrr, store_sem,
):
    row = lax.axis_index("row")
    col = lax.axis_index("col")
    x = row // 4
    zh = (row // 2) % 2
    k = row % 2
    y = col // 4
    zl = col % 4

    def at(dx=0, dz4=0, dk=0, dy=0, dz=0):
        xx = (x + dx) % 4
        zz = (zh + dz4) % 2
        kk = (k + dk) % 2
        yy = (y + dy) % 4
        ll = (zl + dz) % 4
        return {"row": xx * 4 + zz * 2 + kk, "col": yy * 4 + ll}

    gg, gu = big.at[0], big.at[1]

    def settle(sem, ref):
        pltpu.make_async_copy(ref, ref, sem).wait()

    def remote(src, dst, ssem, rsem, device):
        copy = pltpu.make_async_remote_copy(
            src_ref=src, dst_ref=dst, send_sem=ssem, recv_sem=rsem,
            device_id=device, device_id_type=pl.DeviceIdType.MESH,
        )
        copy.start()
        return copy

    ins = (tok_in, cot_in)
    for tc in range(2):
        for j in range(STAGES):
            pltpu.make_async_copy(
                ins[tc].at[pl.ds(16 * j, 16)],
                panel.at[j, tc, zl // 2, y, zl % 2],
                load_sem.at[3],
            ).start()
    loads = []
    for i, (src, dst) in enumerate(((wg_in, wg), (wu_in, wu), (wd_in, wd))):
        loads.append(pltpu.make_async_copy(src, dst.at[0], load_sem.at[i]))
        loads[-1].start()

    barrier = pltpu.get_barrier_semaphore()
    peers = [at(dk=1), at(dz4=1)]
    peers += [at(dx=d) for d in (1, 2, 3)]
    peers += [at(dy=d) for d in (1, 2, 3)]
    peers += [at(dz=d) for d in (1, 2, 3)]
    for peer in peers:
        pl.semaphore_signal(barrier, inc=1, device_id=peer, device_id_type=pl.DeviceIdType.MESH)
    pl.semaphore_wait(barrier, len(peers))

    def tile(j, tc, t):
        ll = (zl - t + 4) % 4
        return panel.at[j, tc, ll // 2, y, ll % 2]

    def send_z(j, tc):
        for d in (1, 3, 2):
            remote(
                ins[tc].at[pl.ds(16 * j, 16)], tile(j, tc, 0),
                azs, azr0.at[tc, d - 1] if j == 0 else azr.at[j, tc], at(dz=d),
            )

    def send_y_tile(tc, t):
        src = tile(0, tc, t) if t else ins[tc].at[pl.ds(0, 16)]
        for d in (2, 1, 3):
            remote(src, tile(0, tc, t), ats, atr.at[tc], at(dy=d))

    wx = []

    def send_weights():
        for i, (src, dst) in enumerate(((wg_in, wg), (wu_in, wu), (wd_in, wd))):
            wx.append(remote(src, dst.at[1], wsend.at[i], wrecv.at[i], at(dk=1)))

    def own_tiles():
        settle(load_sem.at[3], rs_z.at[0])

    def gather_y(j, tc):
        if j == 0:
            for t in (1, 3, 2):
                settle(azr0.at[tc, t - 1], tile(j, tc, t))
                send_y_tile(tc, t)
            return
        settle(azr.at[j, tc], rs_z.at[j, tc])
        for d in (2, 1, 3):
            remote(
                panel.at[j, tc, :, y], panel.at[j, tc, :, y], ays, ayr.at[j, tc], at(dy=d),
            )

    def forward_core(j, tc):
        settle(atr.at[tc] if j == 0 else ayr.at[j, tc], rs_z.at[pl.ds(0, 2)])
        remote(panel.at[j, tc, 1 - k], other.at[j, tc], afs, afr.at[j, tc], at(dk=1))

    def partial(j, a):
        tc = 0 if a < 2 else 1
        if a != 1:
            settle(afr.at[j, tc], other.at[j, tc])
        if j == 0:
            loads[a].wait()
            wx[a].wait_recv()
        lhs0 = panel[j, tc, k].reshape(128, 384)
        lhs1 = other[j, tc].reshape(128, 384)
        w = (wg, wu, wd)[a]
        if a < 2:
            res = dot(lhs0, w[0], ((1,), (0,))) + dot(lhs1, w[1], ((1,), (0,)))
        else:
            res = dot(lhs0, w[0], ((1,), (1,))) + dot(lhs1, w[1], ((1,), (1,)))
        part_own[j, a] = res.reshape(4, 32, 896)
        part[j, a] = res.astype(BF16).reshape(4, 32, 896)
        for d in (2, 1, 3):
            remote(
                part.at[j, a, (x + d) % 4], rs_x.at[j, a, d - 1], xrs, xrr.at[j, a], at(dx=d),
            )

    def sum_x(j, a):
        settle(xrr.at[j, a], rs_x.at[j, a])
        total = part_own[j, a, x]
        for d in (1, 2, 3):
            total = total + rs_x[j, a, d - 1].astype(F32)
        part_own[j, a, x] = total
        zs[j, a] = total.astype(BF16)
        remote(zs.at[j, a], zr.at[j, a], z4s, z4r.at[j, a], at(dz4=1))

    def spread(j, a, value):
        hid[j, a, k, x] = value.astype(BF16)
        for d in (1, 3):
            remote(
                hid.at[j, a, k, x], hid.at[j, a, k, x], xas, xar.at[j, a, d // 2], at(dx=d),
            )

    def gate_up(j):
        return tuple(part_own[j, a, x] + zr[j, a].astype(F32) for a in range(2))

    def forward(j):
        settle(z4r.at[j, 0], zr.at[j, 0])
        settle(z4r.at[j, 1], zr.at[j, 1])
        gate, up = gate_up(j)
        spread(j, 0, gate * jax.nn.sigmoid(gate) * up)

    def backward(j):
        settle(z4r.at[j, 2], zr.at[j, 2])
        gate, up = gate_up(j)
        sig = jax.nn.sigmoid(gate)
        d_hidden = part_own[j, 2, x] + zr[j, 2].astype(F32)
        spread(j, 1, d_hidden * up * sig * (1.0 + gate * (1.0 - sig)))
        spread(j, 2, d_hidden * gate * sig)

    def relay(j, a):
        for d, half in ((1, 0), (3, 1)):
            settle(xar.at[j, a, half], hid.at[j, a, k, (x + 4 - d) % 4])
            piece = hid.at[j, a, k, (x + 4 - d) % 4, pl.ds(16 * half, 16)]
            remote(piece, piece, xas, xbr.at[j, a], at(dx=d))

    def forward_hidden(j, a):
        settle(xbr.at[j, a], hid.at[j, a, k, (x + 2) % 4])
        remote(hid.at[j, a, k], hid.at[j, a, k], hfs, hfr.at[j, a], at(dk=1))

    def stage_hidden(j, a):
        return hid[j, a].reshape(256, 896)

    def send_y(j, b, res):
        res = res.reshape(2, 4, 32, 384)
        oparts_own[j, b] = res
        oparts[j, b] = res.astype(BF16)
        for d in (2, 1, 3):
            remote(
                oparts.at[j, b, :, (y + d) % 4], rs_y.at[j, b, d - 1], yrs, yrr.at[j, b], at(dy=d),
            )

    def project(j, b):
        if b == 0:
            settle(hfr.at[j, 0], hid.at[j, 0, 1 - k])
            send_y(j, 0, dot(stage_hidden(j, 0), wd[0], ((1,), (0,))))
        else:
            settle(hfr.at[j, 1], hid.at[j, 1, 1 - k])
            settle(hfr.at[j, 2], hid.at[j, 2, 1 - k])
            send_y(j, 1, dot(stage_hidden(j, 1), wg[0], ((1,), (1,)))
                   + dot(stage_hidden(j, 2), wu[0], ((1,), (1,))))

    def grads(j, i):
        tok = panel[j, 0].reshape(256, 384)
        cot = panel[j, 1].reshape(256, 384)
        acc, l, r = (
            (gg, tok, stage_hidden(j, 1)),
            (gu, tok, stage_hidden(j, 2)),
            (gd, stage_hidden(j, 0), cot),
        )[i]
        term = dot(l, r, ((0,), (0,)))
        if j > 0:
            term = acc[...] + term
        if j == STAGES - 1:
            term = term * scale
        acc[...] = term

    def sum_y(j, b):
        settle(yrr.at[j, b], rs_y.at[j, b])
        total = oparts_own[j, b, :, y]
        for d in (1, 2, 3):
            total = total + rs_y[j, b, d - 1].astype(F32)
        oparts_own[j, b, :, y] = total
        zout[j, b] = total.astype(zout.dtype).reshape(4, 16, 384)
        for d in (2, 1, 3):
            remote(
                zout.at[j, b, (zl + d) % 4], rs_z.at[j, b, d - 1], zrs, zrr.at[j, b], at(dz=d),
            )

    def finish(j, b):
        settle(zrr.at[j, b], rs_z.at[j, b])
        total = oparts_own[j, b, zl // 2, y, pl.ds(pl.multiple_of(zl % 2 * 16, 16), 16)]
        for d in (1, 2, 3):
            total = total + rs_z[j, b, d - 1].astype(F32)
        (out_ref, gin_ref)[b][pl.ds(16 * j, 16)] = total.astype(BF16)

    def store(i):
        src = (out_ref, gin_ref, gg, gu, gd)[i]
        dst = (out_any, gin_any, gg_any, gu_any, gd_any)[i]
        pltpu.make_async_copy(src, dst, store_sem.at[(0, 0, 1, 1, 2)[i]]).start()

    steps = (
        (send_z, 0, 0), (send_y_tile, 0, 0), (send_z, 0, 1), (send_y_tile, 1, 0), (send_weights,),
        (send_z, 1, 0), (send_z, 1, 1), (send_z, 2, 0), (send_z, 2, 1),
        (gather_y, 0, 0), (gather_y, 0, 1), (own_tiles,), (gather_y, 1, 0), (forward_core, 0, 0), (gather_y, 1, 1),
        (partial, 0, 0), (partial, 0, 1), (forward_core, 0, 1), (gather_y, 2, 0), (gather_y, 2, 1),
        (forward_core, 1, 0), (partial, 0, 2), (forward_core, 1, 1), (partial, 1, 0), (partial, 1, 1), (partial, 1, 2),
        (sum_x, 0, 0), (sum_x, 0, 1), (forward_core, 2, 0), (forward_core, 2, 1), (partial, 2, 0), (partial, 2, 1), (partial, 2, 2),
        (sum_x, 0, 2), (sum_x, 1, 0), (forward, 0), (sum_x, 1, 1), (backward, 0), (sum_x, 1, 2), (sum_x, 2, 0), (forward, 1),
        (sum_x, 2, 1), (backward, 1), (sum_x, 2, 2),
        (relay, 0, 0), (relay, 0, 1), (forward, 2), (relay, 0, 2), (forward_hidden, 0, 0), (relay, 1, 0), (backward, 2),
        (forward_hidden, 0, 1), (relay, 1, 1), (forward_hidden, 0, 2), (relay, 1, 2), (forward_hidden, 1, 0),
        (project, 0, 0), (project, 0, 1), (grads, 0, 0), (relay, 2, 0), (forward_hidden, 1, 1), (forward_hidden, 1, 2),
        (grads, 0, 1), (grads, 0, 2), (project, 1, 0), (relay, 2, 1), (project, 1, 1), (relay, 2, 2), (sum_y, 0, 0), (sum_y, 0, 1),
        (forward_hidden, 2, 0), (project, 2, 0), (forward_hidden, 2, 1), (forward_hidden, 2, 2),
        (project, 2, 1), (sum_y, 1, 0), (sum_y, 1, 1), (grads, 1, 0), (grads, 1, 1), (grads, 1, 2), (finish, 0, 0), (finish, 0, 1),
        (sum_y, 2, 0), (grads, 2, 2), (store, 4), (grads, 2, 0), (store, 2), (grads, 2, 1), (store, 3), (sum_y, 2, 1),
        (finish, 1, 0), (finish, 1, 1), (finish, 2, 0), (store, 0), (finish, 2, 1), (store, 1),
    )
    for step, *where in steps:
        step(*where)
    settle(store_sem.at[0], rs_z.at[0])
    settle(store_sem.at[1], big)
    settle(store_sem.at[2], gd)
    for i, ref in enumerate((wg, wu, wd)):
        settle(wsend.at[i], ref.at[1])
    settle(azs, rs_z)
    settle(ats, zout)
    settle(ays, other)
    settle(afs, other)
    settle(xrs, rs_x)
    settle(z4s, zs)
    settle(xas, rs_x)
    settle(hfs, part)
    settle(yrs, rs_y)
    settle(zrs, rs_z)


def write_out(*refs):
    copies = [pltpu.make_async_copy(refs[i], refs[5 + i], refs[10].at[i]) for i in range(5)]
    for copy in copies:
        copy.start()
    for copy in copies:
        copy.wait()


def body(tokens, gate_weight, up_weight, down_weight, cotangent):
    total_tokens = tokens.shape[0] * lax.axis_size("col")
    scale = total_tokens ** (-0.5)
    vmem = pl.BlockSpec(memory_space=pltpu.VMEM)
    hbm = pl.BlockSpec(memory_space=pl.ANY)
    S = STAGES
    sem = pltpu.SemaphoreType.DMA
    scratch = [
        pltpu.VMEM((S, 2, 2, 4, 2, 16, 384), BF16),
        pltpu.VMEM((S, 2, 4, 2, 16, 384), BF16),
        pltpu.VMEM((2, 384, 896), BF16),
        pltpu.VMEM((2, 384, 896), BF16),
        pltpu.VMEM((2, 896, 384), BF16),
        pltpu.VMEM((S, 3, 4, 32, 896), BF16),
        pltpu.VMEM((S, 3, 4, 32, 896), F32),
        pltpu.VMEM((S, 3, 3, 32, 896), BF16),
        pltpu.VMEM((S, 3, 32, 896), BF16),
        pltpu.VMEM((S, 3, 32, 896), BF16),
        pltpu.VMEM((S, 3, 2, 4, 32, 896), BF16),
        pltpu.VMEM((S, 2, 2, 4, 32, 384), BF16),
        pltpu.VMEM((S, 2, 2, 4, 32, 384), F32),
        pltpu.VMEM((S, 2, 3, 2, 32, 384), BF16),
        pltpu.VMEM((S, 2, 4, 16, 384), BF16),
        pltpu.VMEM((S, 2, 3, 16, 384), BF16),
        pltpu.VMEM((48, 384), BF16),
        pltpu.VMEM((48, 384), BF16),
        pltpu.VMEM((2, 384, 896), F32),
        pltpu.VMEM((896, 384), F32),
        sem((4,)), sem((3,)), sem((3,)),
        sem(()), sem((S, 2)), sem((2, 3)), sem(()), sem((2,)), sem(()), sem((S, 2)), sem(()), sem((S, 2)),
        sem(()), sem((S, 3)), sem(()), sem((S, 3)), sem(()), sem((S, 3, 2)), sem((S, 3)), sem(()), sem((S, 3)),
        sem(()), sem((S, 2)), sem(()), sem((S, 2)), sem((3,)),
    ]
    results = pl.pallas_call(
        functools.partial(kernel, scale),
        out_shape=(
            pltpu.VMEM((48, 384), BF16),
            pltpu.VMEM((48, 384), BF16),
            pltpu.VMEM((384, 896), F32),
            pltpu.VMEM((384, 896), F32),
            pltpu.VMEM((896, 384), F32),
        ),
        in_specs=[pl.BlockSpec(memory_space=pltpu.HBM)] * 5,
        out_specs=(hbm,) * 5,
        scratch_shapes=scratch,
        compiler_params=pltpu.CompilerParams(
            collective_id=0, has_side_effects=True, vmem_limit_bytes=36 * 1024 * 1024,
        ),
        cost_estimate=pl.CostEstimate(
            flops=2 * 9 * 768 * 384 * 896, bytes_accessed=8 * 1024 * 1024, transcendentals=0,
        ),
        name="ffn",
    )(*(
        pltpu.with_memory_space_constraint(a, pltpu.HBM)
        for a in (tokens, gate_weight, up_weight, down_weight, cotangent)
    ))
    return pl.pallas_call(
        write_out,
        out_shape=tuple(jax.ShapeDtypeStruct(r.shape, r.dtype) for r in results),
        in_specs=[vmem] * 5,
        out_specs=(hbm,) * 5,
        scratch_shapes=[sem((5,))],
        compiler_params=pltpu.CompilerParams(vmem_limit_bytes=1024 * 1024),
        name="write_out",
    )(*results)


def solution(mesh):
    return jax.shard_map(
        body,
        mesh=mesh,
        in_specs=(
            P("col", "row"),
            P("row", "col"),
            P("row", "col"),
            P("col", "row"),
            P("col", "row"),
        ),
        out_specs=(
            P("col", "row"),
            P("col", "row"),
            P("row", "col"),
            P("row", "col"),
            P("col", "row"),
        ),
        check_vma=False,
    )
```

time: 571 us -> 79.1 us (0.14); the launches traced: 560 us -> 79.1 us
  waiting for transfers between devices: 434 us -> 0 us
  blocking collectives: 79.7 us -> 0 us
  Pallas kernels: 0 us -> 78.4 us
  matrix products: 19.8 us -> 0 us
  between operations: 14.2 us -> 0.64 us
  other arithmetic: 8.28 us -> 0 us
    reduce_scatter x4 -> x0, waiting for transfers between devices: 313 us -> none  [the longest x2 169 us: share_total(): return lax.psum_scatter(stacked, 'row', scatter_dimension=1, tiled=True)]
    all_gather x2 -> x0, waiting for transfers between devices: 120 us -> none  [share_gather(): return lax.all_gather(stacked, 'row', axis=1, tiled=True)]
    all_gather x2 -> x0, blocking collectives: 79.7 us -> none  [token_panel(): return lax.all_gather(piece, 'col', axis=0, tiled=True)]
    pallas_call x0 -> x2, Pallas kernels: none -> 78.4 us  [the longest x1 76.4 us: body(): pl.pallas_call(functools.partial(kernel, scale), out_shape=(pltpu.VMEM((4...]
    dot_general x9 -> x0, matrix products: 19.8 us -> none  [the longest x3 7.8 us: contract_first(): lax.dot_general(left, right, (((0,), (0,)), ((), ())), preferred_element_...]
  transfers between devices with their start and end apart: 6 -> 0, of which waited for: 6 -> 0; matrix products, arithmetic and copies ran while one was open for 5% -> 0% of each run, Pallas kernels for 0% -> 0%
where the time goes in v2:
time: 79.1 us
  Pallas kernels  78.4 us (99%)
    pallas_call x1, Pallas kernels, body(): pl.pallas_call(functools.partial(kernel, scale), out_shape=(pltpu.VMEM((4...  76.4 us
    pallas_call x1, Pallas kernels, body(): pl.pallas_call(write_out, out_shape=tuple((jax.ShapeDtypeStruct(r.shape,...  2.06 us

profile of v2, /device:TPU:1, one launch (start us, length us, event | category | flops | bytes accessed | tf_op | source)
XLA Modules:
  0.0 79.1 jit_solution(14142232532548660131)
XLA Ops:
  0.6 76.4 %ffn.1 = (bf16[48,384]{1,0:T(8,128)(2,1)S(1)}, bf16[48,384]{1,0:T(8,128)(2,1)S(1)}, f32[384,896]{1,0:T(8,128)S(1)}, f32[384,896]{1,0:T(8,128)S(1)}, f32[896,384]{1,0:T(8,128)S(1)}) custom-call(bf16[48,384]{1,0:T(8,128)(2,1)} %tok_in.1, bf16[384,896]{1,0:T(8,128)(2,1)} %wg_in.1, bf16[384,896]{1,0:T(8,128)(2,1)} %wu_in.1, bf16[896,384]{1,0:T(8,128)(2,1)} %wd_in.1, ...), custom_call_target="tpu_custom_call" | custom-call | flops 4756340736 | bytes 8388608 | tf_op jit(solution)/shard_map/ffn/pallas_call | solution.py:327
  77.0 2.1 %write_out.1 = (bf16[48,384]{1,0:T(8,128)(2,1)}, bf16[48,384]{1,0:T(8,128)(2,1)}, f32[384,896]{1,0:T(8,128)}, f32[384,896]{1,0:T(8,128)}, f32[896,384]{1,0:T(8,128)}) custom-call(bf16[48,384]{1,0:T(8,128)(2,1)S(1)} %get-tuple-element.10.refs_0_, bf16[48,384]{1,0:T(8,128)(2,1)S(1)} %get-tuple-element.11.refs_1_, f32[384,896]{1,0:T(8,128)S(1)} %get-tuple-element.12.refs_2_, ...), custom_call_target="tpu_custom_call" | custom-call | tf_op jit(solution)/shard_map/write_out/pallas_call | solution.py:350

commit v3 on v2

v3 whole, which is shorter than its diff:
```python
import functools

import jax
import jax.numpy as jnp
from jax import lax
from jax.experimental import pallas as pl
from jax.experimental.pallas import tpu as pltpu
from jax.sharding import PartitionSpec as P

TILES = 3
STRAIGHT = (0,)
WHOLE = (3,)
BF16 = jnp.bfloat16
F32 = jnp.float32


def dot(a, b, dims):
    return lax.dot_general(a, b, (dims, ((), ())), preferred_element_type=F32)


STRIPS = (
    ((0, 0), (0, 1)),
    ((1, 0), (1, 1), (3, 0), (3, 1)),
    ((0, 2), (1, 2), (3, 2), (2, 0)),
    ((2, 1), (2, 2)),
)
STAGES = len(STRIPS)
SMALL = (0, 3)


def kernel(
    scale,
    tok_in, wg_in, wu_in, wd_in, cot_in,
    out_any, gin_any, gg_any, gu_any, gd_any,
    panel, other, wg, wu, wd,
    part_s, part_l, own_s, own_l, pairs_s, pairs_l, rs_x_s, rs_x_l, zs_s, zs_l, zr_s, zr_l, hid_s, hid_l,
    oparts, oparts_own, rs_y, zout, zout_b, rs_z, rs_z_b,
    out_ref, gin_ref, big, gd,
    load_sem, wsend, wrecv,
    azs, azr, azr_b, ats, atr, ays, ayr, ayr_b, afs, afr,
    xrs, xpr, xrr, z4s, z4r, xas, xar, xbr, hfs, hfr,
    yrs, yrr, zrs, zrr, store_sem,
):
    row = lax.axis_index("row")
    col = lax.axis_index("col")
    x = row // 4
    zh = (row // 2) % 2
    k = row % 2
    y = col // 4
    zl = col % 4
    turn = 1 + 2 * k

    def at(dx=0, dz4=0, dk=0, dy=0, dz=0):
        xx = (x + dx) % 4
        zz = (zh + dz4) % 2
        kk = (k + dk) % 2
        yy = (y + dy) % 4
        ll = (zl + dz) % 4
        return {"row": xx * 4 + zz * 2 + kk, "col": yy * 4 + ll}

    def pick(s, small, large):
        return small.at[SMALL.index(s)] if s in SMALL else large.at[s - 1]

    def kind(s):
        return 0 if s in SMALL else 1

    part = [pick(s, part_s, part_l) for s in range(STAGES)]
    part_own = [pick(s, own_s, own_l) for s in range(STAGES)]
    pairs = [pick(s, pairs_s, pairs_l) for s in range(STAGES)]
    rs_x = [pick(s, rs_x_s, rs_x_l) for s in range(STAGES)]
    zs = [pick(s, zs_s, zs_l) for s in range(STAGES)]
    zr = [pick(s, zr_s, zr_l) for s in range(STAGES)]
    hid = [pick(s, hid_s, hid_l) for s in range(STAGES)]
    gg, gu = big.at[0], big.at[1]

    def settle(sem, ref):
        pltpu.make_async_copy(ref, ref, sem).wait()

    def remote(src, dst, ssem, rsem, device):
        copy = pltpu.make_async_remote_copy(
            src_ref=src, dst_ref=dst, send_sem=ssem, recv_sem=rsem,
            device_id=device, device_id_type=pl.DeviceIdType.MESH,
        )
        copy.start()
        return copy

    ins = (tok_in, cot_in)
    first, last = pl.ds(0, 2), pl.ds(2, 1)
    for tc in range(2):
        pltpu.make_async_copy(ins[tc], panel.at[:, tc, zl // 2, y, zl % 2], load_sem.at[3]).start()
    loads = []
    for i, (src, dst) in enumerate(((wg_in, wg), (wu_in, wu), (wd_in, wd))):
        loads.append(pltpu.make_async_copy(src, dst.at[0], load_sem.at[i]))
        loads[-1].start()

    barrier = pltpu.get_barrier_semaphore()
    peers = [at(dk=1), at(dz4=1)]
    peers += [at(dx=d) for d in (1, 2, 3)]
    peers += [at(dy=d) for d in (1, 2, 3)]
    peers += [at(dz=d) for d in (1, 2, 3)]
    for peer in peers:
        pl.semaphore_signal(barrier, inc=1, device_id=peer, device_id_type=pl.DeviceIdType.MESH)
    pl.semaphore_wait(barrier, len(peers))

    def tiles(js, tc, t):
        ll = (zl - t + 4) % 4
        return panel.at[js, tc, ll // 2, y, ll % 2]

    def send_z(late, tc):
        js = last if late else first
        for d in (1, 3, 2):
            remote(
                ins[tc].at[js], tiles(js, tc, 0),
                azs, azr_b.at[tc] if late else azr.at[tc, d - 1], at(dz=d),
            )

    def send_near(tc, t):
        src = tiles(first, tc, t) if t else ins[tc].at[first]
        for d in (1, 3):
            remote(src, tiles(first, tc, t), ats, atr.at[tc], at(dy=d))

    wx = []

    def send_weights():
        for i, (src, dst) in enumerate(((wg_in, wg), (wu_in, wu), (wd_in, wd))):
            wx.append(remote(src, dst.at[1], wsend.at[i], wrecv.at[i], at(dk=1)))

    def own_tiles():
        settle(load_sem.at[3], other.at[:, :, 0, 0])

    def gather_near(tc):
        for t in (1, 3, 2):
            settle(azr.at[tc, t - 1], tiles(first, tc, t))
            send_near(tc, t)

    def gather_last(tc):
        settle(azr_b.at[tc], other.at[0, tc, pl.ds(0, 3), 0])
        block = panel.at[last, tc, :, y]
        for d in (1, 3):
            remote(block, block, ays.at[0], ayr_b.at[tc, 0], at(dy=d))

    def gather_far(tc):
        block = panel.at[pl.ds(0, 1), tc, :, y]
        remote(block, block, ays.at[0], ayr.at[tc], at(dy=2))

    def gather_end(tc):
        block = panel.at[pl.ds(1, 2), tc, :, y]
        remote(block, block, ays.at[1], ayr_b.at[tc, 1], at(dy=2))

    def forward_core(s, tc):
        if s == 1:
            settle(atr.at[tc], other.at[0])
        if s == 2:
            settle(ayr_b.at[tc, 0], other.at[0, tc])
            settle(ayr.at[tc], other.at[0, tc, pl.ds(0, 2)])
        if s == 3:
            settle(ayr_b.at[tc, 1], other.at[0, tc])
        for dy in sorted({dy for dy, _ in STRIPS[s]}):
            js = [j for d, j in STRIPS[s] if d == dy]
            js = pl.ds(js[0], len(js))
            yy = (y + dy) % 4
            remote(panel.at[js, tc, 1 - k, yy], other.at[js, tc, yy], afs, afr.at[s, tc], at(dk=1))

    def partial(s, a):
        tc = 0 if a < 2 else 1
        n = len(STRIPS[s])
        if a != 1:
            settle(afr.at[s, tc], other.at[0, tc, pl.ds(0, n)])
        if s == 0:
            loads[a].wait()
            wx[a].wait_recv()
        lhs0 = jnp.concatenate([panel[j, tc, k, (y + dy) % 4].reshape(32, 384) for dy, j in STRIPS[s]])
        lhs1 = jnp.concatenate([other[j, tc, (y + dy) % 4].reshape(32, 384) for dy, j in STRIPS[s]])
        w = (wg, wu, wd)[a]
        if a < 2:
            res = dot(lhs0, w[0], ((1,), (0,))) + dot(lhs1, w[1], ((1,), (0,)))
        else:
            res = dot(lhs0, w[0], ((1,), (1,))) + dot(lhs1, w[1], ((1,), (1,)))
        part_own[s][a] = res.reshape(4, 8 * n, 896)
        part[s][a] = res.astype(BF16).reshape(4, 8 * n, 896)
        ssem = xrs.at[kind(s)]
        if s in STRAIGHT:
            if s in SMALL:
                remote(part[s].at[a, (x + 2) % 4], pairs[s].at[a, 0], ssem, xpr.at[s, a, 0], at(dx=2))
            else:
                for i in range(2):
                    remote(part[s].at[a, (x + 2) % 4, pl.ds(16 * i, 16)], pairs[s].at[a, i],
                           ssem, xpr.at[s, a, i], at(dx=2))
            for i, d in enumerate((1, 3)):
                remote(part[s].at[a, (x + d) % 4], rs_x[s].at[a, i], ssem, xrr.at[s, a], at(dx=d))
        elif s in SMALL:
            remote(part[s].at[a, (x + 2) % 4], pairs[s].at[a, 0], ssem, xpr.at[s, a, 0], at(dx=turn))
            remote(part[s].at[a, (x + 4 - turn) % 4], rs_x[s].at[a, 1], ssem, xrr.at[s, a], at(dx=4 - turn))
        else:
            for i, d in enumerate((1, 3)):
                remote(part[s].at[a, (x + 2) % 4, pl.ds(16 * i, 16)], pairs[s].at[a, i],
                       ssem, xpr.at[s, a, i], at(dx=d))
            for i, d in enumerate((1, 3)):
                rows = pl.ds(16 - 16 * i, 16)
                remote(part[s].at[a, (x + d) % 4, rows], rs_x[s].at[a, i, rows], ssem, xrr.at[s, a], at(dx=d))

    def pass_on(s, a):
        ssem = xrs.at[kind(s)]
        if s in SMALL:
            settle(xpr.at[s, a, 0], pairs[s].at[a, 0])
            both = part_own[s][a, (x + turn) % 4] + pairs[s][a, 0].astype(F32)
            part[s][a, (x + turn) % 4] = both.astype(BF16)
            remote(part[s].at[a, (x + turn) % 4], rs_x[s].at[a, 0], ssem, xrr.at[s, a], at(dx=turn))
            return
        for i, d in enumerate((1, 3)):
            settle(xpr.at[s, a, i], pairs[s].at[a, i])
            rows = pl.ds(16 * i, 16)
            both = part_own[s][a, (x + d) % 4, rows] + pairs[s][a, i].astype(F32)
            part[s][a, (x + d) % 4, rows] = both.astype(BF16)
            remote(part[s].at[a, (x + d) % 4, rows], rs_x[s].at[a, i, rows], ssem, xrr.at[s, a], at(dx=d))

    def sum_x(s, a):
        settle(xrr.at[s, a], rs_x[s].at[a])
        total = part_own[s][a, x] + rs_x[s][a, 0].astype(F32) + rs_x[s][a, 1].astype(F32)
        if s in STRAIGHT:
            for i in range(1 if s in SMALL else 2):
                settle(xpr.at[s, a, i], pairs[s].at[a, i])
            total = total + pairs[s][a].reshape(total.shape).astype(F32)
        part_own[s][a, x] = total
        zs[s][a] = total.astype(BF16)
        remote(zs[s].at[a], zr[s].at[a], z4s.at[kind(s)], z4r.at[s, a], at(dz4=1))

    def spread(s, a, value):
        hid[s][a, k, x] = value.astype(BF16)
        piece = hid[s].at[a, k, x]
        if s in WHOLE:
            remote(piece, piece, xas.at[kind(s)], xbr.at[s, a], at(dx=2))
        for d in (1, 3):
            remote(piece, piece, xas.at[kind(s)], xar.at[s, a, d // 2], at(dx=d))

    def gate_up(s):
        return tuple(part_own[s][a, x] + zr[s][a].astype(F32) for a in range(2))

    def forward(s):
        settle(z4r.at[s, 0], zr[s].at[0])
        settle(z4r.at[s, 1], zr[s].at[1])
        gate, up = gate_up(s)
        spread(s, 0, gate * jax.nn.sigmoid(gate) * up)

    def backward(s):
        settle(z4r.at[s, 2], zr[s].at[2])
        gate, up = gate_up(s)
        sig = jax.nn.sigmoid(gate)
        d_hidden = part_own[s][2, x] + zr[s][2].astype(F32)
        spread(s, 1, d_hidden * up * sig * (1.0 + gate * (1.0 - sig)))
        spread(s, 2, d_hidden * gate * sig)

    def relay(s, a):
        if s in SMALL:
            for i, d in enumerate((1, 3)):
                settle(xar.at[s, a, i], hid[s].at[a, k, (x + 4 - d) % 4])
            piece = hid[s].at[a, k, (x + 4 - turn) % 4]
            remote(piece, piece, xas.at[0], xbr.at[s, a], at(dx=turn))
            return
        for i, d in enumerate((1, 3)):
            settle(xar.at[s, a, i], hid[s].at[a, k, (x + 4 - d) % 4])
            piece = hid[s].at[a, k, (x + 4 - d) % 4, pl.ds(16 * i, 16)]
            remote(piece, piece, xas.at[1], xbr.at[s, a], at(dx=d))

    def forward_hidden(s, a):
        if s in WHOLE:
            for i, d in enumerate((1, 3)):
                settle(xar.at[s, a, i], hid[s].at[a, k, (x + 4 - d) % 4])
        settle(xbr.at[s, a], hid[s].at[a, k, (x + 2) % 4])
        remote(hid[s].at[a, k], hid[s].at[a, k], hfs.at[kind(s)], hfr.at[s, a], at(dk=1))

    def take(s, a):
        settle(hfr.at[s, a], hid[s].at[a, 1 - k])

    def project(s, b, other_core):
        n = len(STRIPS[s])
        kk = 1 - k if other_core else k
        if b == 0:
            res = dot(hid[s][0, kk].reshape(32 * n, 896), wd[0], ((1,), (0,)))
        else:
            res = (dot(hid[s][1, kk].reshape(32 * n, 896), wg[0], ((1,), (1,)))
                   + dot(hid[s][2, kk].reshape(32 * n, 896), wu[0], ((1,), (1,))))
        res = res.reshape(n, 32, 384)
        for i, (dy, j) in enumerate(STRIPS[s]):
            oparts_own[j, b, kk, (y + dy) % 4] = res[i]
            if dy:
                oparts[j, b, kk, (y + dy) % 4] = res[i].astype(BF16)
                remote(
                    oparts.at[j, b, kk, (y + dy) % 4], rs_y.at[j, b, dy - 1, kk],
                    yrs, yrr.at[j, b], at(dy=dy),
                )

    def grads(s, i):
        n = len(STRIPS[s])

        def rows(tc):
            return jnp.concatenate(
                [panel[j, tc, kk, (y + dy) % 4].reshape(32, 384) for kk in range(2) for dy, j in STRIPS[s]]
            )

        def units(a):
            return hid[s][a].reshape(64 * n, 896)

        if i < 2:
            acc, term = (gg, gu)[i], dot(rows(0), units(1 + i), ((0,), (0,)))
        else:
            acc, term = gd, dot(units(0), rows(1), ((0,), (0,)))
        if s > 0:
            term = acc[...] + term
        if s == STAGES - 1:
            term = term * scale
        acc[...] = term

    def sums(j):
        return (zout_b, rs_z_b, j - 1, zrs.at[1]) if j else (zout, rs_z, 0, zrs.at[0])

    def sum_y(j, b):
        settle(yrr.at[j, b], rs_y.at[j, b])
        total = oparts_own[j, b, :, y]
        for d in (1, 2, 3):
            total = total + rs_y[j, b, d - 1].astype(F32)
        oparts_own[j, b, :, y] = total
        mine, theirs, i, ssem = sums(j)
        mine[i, b] = total.astype(mine.dtype).reshape(4, 16, 384)
        for d in (2, 1, 3):
            remote(mine.at[i, b, (zl + d) % 4], theirs.at[i, b, d - 1], ssem, zrr.at[j, b], at(dz=d))

    def finish(j, b):
        mine, theirs, i, ssem = sums(j)
        settle(zrr.at[j, b], theirs.at[i, b])
        total = oparts_own[j, b, zl // 2, y, pl.ds(pl.multiple_of(zl % 2 * 16, 16), 16)]
        for d in (1, 2, 3):
            total = total + theirs[i, b, d - 1].astype(F32)
        (out_ref, gin_ref)[b][pl.ds(16 * j, 16)] = total.astype(BF16)

    def store(i):
        src = (out_ref, gin_ref, gg, gu, gd)[i]
        dst = (out_any, gin_any, gg_any, gu_any, gd_any)[i]
        pltpu.make_async_copy(src, dst, store_sem.at[(0, 0, 1, 1, 2)[i]]).start()

    steps = (
        (send_z, 0, 0), (send_near, 1, 0), (send_z, 1, 0), (own_tiles,), (send_near, 0, 0), (send_weights,),
        (send_z, 0, 1), (gather_near, 0), (forward_core, 0, 0), (gather_last, 0), (send_z, 1, 1), (partial, 0, 0),
        (gather_near, 1), (forward_core, 0, 1), (partial, 0, 1), (forward_core, 1, 0), (gather_far, 0),
        (gather_end, 0), (partial, 0, 2), (partial, 1, 0), (partial, 1, 1), (sum_x, 0, 0), (forward_core, 1, 1),
        (sum_x, 0, 1), (sum_x, 0, 2), (gather_far, 1), (forward_core, 2, 0), (gather_last, 1), (pass_on, 1, 0),
        (gather_end, 1), (partial, 1, 2), (forward_core, 3, 0), (pass_on, 1, 1), (partial, 2, 0), (partial, 2, 1),
        (sum_x, 1, 0), (pass_on, 1, 2), (forward_core, 2, 1), (sum_x, 1, 1), (forward, 0), (partial, 3, 0),
        (pass_on, 2, 0), (pass_on, 2, 1), (partial, 2, 2), (sum_x, 1, 2), (partial, 3, 1), (backward, 0),
        (forward_core, 3, 1), (sum_x, 2, 0), (pass_on, 2, 2), (sum_x, 2, 1), (relay, 0, 0), (partial, 3, 2),
        (pass_on, 3, 0), (pass_on, 3, 1), (forward, 1), (relay, 0, 2), (relay, 0, 1), (sum_x, 2, 2), (pass_on, 3, 2),
        (backward, 1), (sum_x, 3, 0), (relay, 1, 0), (forward_hidden, 0, 0), (forward_hidden, 0, 1),
        (forward_hidden, 0, 2), (sum_x, 3, 1), (project, 0, 1, 0), (sum_x, 3, 2), (relay, 1, 1), (relay, 1, 2),
        (forward, 2), (forward_hidden, 1, 0), (backward, 2), (take, 0, 1), (forward_hidden, 1, 1), (take, 1, 0),
        (take, 0, 2), (forward_hidden, 1, 2), (project, 1, 1, 0), (project, 1, 0, 1), (relay, 2, 0), (forward, 3),
        (project, 1, 0, 0), (backward, 3), (grads, 0, 0), (take, 1, 1), (take, 1, 2), (project, 1, 1, 1),
        (relay, 2, 1), (relay, 2, 2), (forward_hidden, 2, 0), (project, 2, 0, 0), (forward_hidden, 3, 0),
        (project, 3, 0, 0), (take, 0, 0), (project, 0, 1, 1), (take, 2, 0), (project, 2, 0, 1), (project, 0, 0, 1),
        (grads, 0, 2), (take, 3, 0), (project, 3, 0, 1), (forward_hidden, 3, 1), (forward_hidden, 3, 2),
        (project, 3, 1, 0), (forward_hidden, 2, 1), (forward_hidden, 2, 2), (project, 2, 1, 0), (project, 0, 0, 0),
        (take, 3, 2), (take, 3, 1), (project, 3, 1, 1), (take, 2, 1), (grads, 1, 2), (take, 2, 2), (sum_y, 0, 0),
        (project, 2, 1, 1), (grads, 0, 1), (grads, 1, 1), (grads, 2, 1), (sum_y, 1, 0), (sum_y, 2, 0), (grads, 3, 1),
        (grads, 2, 2), (sum_y, 1, 1), (sum_y, 2, 1), (store, 3), (grads, 3, 2), (sum_y, 0, 1), (grads, 1, 0),
        (finish, 2, 0), (finish, 2, 1), (grads, 2, 0), (finish, 1, 1), (grads, 3, 0), (finish, 1, 0), (finish, 0, 0),
        (store, 2), (store, 4), (store, 0), (finish, 0, 1), (store, 1),
    )
    for step, *where in steps:
        step(*where)
    settle(store_sem.at[0], other.at[:, :, 0, 0])
    settle(store_sem.at[1], big)
    settle(store_sem.at[2], gd)
    for i, ref in enumerate((wg, wu, wd)):
        settle(wsend.at[i], ref.at[1])
    settle(azs, other.at[:, :, pl.ds(0, 3), 0])
    settle(ats, other.at[pl.ds(0, 2)])
    settle(ays.at[0], other.at[:, :, :, 0])
    settle(ays.at[1], other.at[0])
    settle(afs, other)
    for i, ref in enumerate((part_s, part_l)):
        settle(xrs.at[i], ref.at[:, :, pl.ds(0, 3)])
        settle(xas.at[i], ref.at[:, :, pl.ds(0, 3)])
        settle(hfs.at[i], ref)
        settle(z4s.at[i], (zs_s, zs_l)[i])
        settle(zrs.at[i], (rs_z, rs_z_b)[i])
    settle(yrs, rs_y)


def write_out(*refs):
    copies = [pltpu.make_async_copy(refs[i], refs[5 + i], refs[10].at[i]) for i in range(5)]
    for copy in copies:
        copy.start()
    for copy in copies:
        copy.wait()


def body(tokens, gate_weight, up_weight, down_weight, cotangent):
    total_tokens = tokens.shape[0] * lax.axis_size("col")
    scale = total_tokens ** (-0.5)
    vmem = pl.BlockSpec(memory_space=pltpu.VMEM)
    hbm = pl.BlockSpec(memory_space=pl.ANY)
    sem = pltpu.SemaphoreType.DMA
    both = lambda *shape, dtype=BF16: [pltpu.VMEM((2, 3, *shape, r, 896), dtype) for r in (16, 32)]
    scratch = [
        pltpu.VMEM((TILES, 2, 2, 4, 2, 16, 384), BF16),
        pltpu.VMEM((TILES, 2, 4, 2, 16, 384), BF16),
        pltpu.VMEM((2, 384, 896), BF16),
        pltpu.VMEM((2, 384, 896), BF16),
        pltpu.VMEM((2, 896, 384), BF16),
        *both(4), *both(4, dtype=F32),
        pltpu.VMEM((2, 3, 1, 16, 896), BF16),
        pltpu.VMEM((2, 3, 2, 16, 896), BF16),
        *both(2), *both(), *both(), *both(2, 4),
        pltpu.VMEM((TILES, 2, 2, 4, 32, 384), BF16),
        pltpu.VMEM((TILES, 2, 2, 4, 32, 384), F32),
        pltpu.VMEM((TILES, 2, 3, 2, 32, 384), BF16),
        pltpu.VMEM((1, 2, 4, 16, 384), F32),
        pltpu.VMEM((2, 2, 4, 16, 384), BF16),
        pltpu.VMEM((1, 2, 3, 16, 384), F32),
        pltpu.VMEM((2, 2, 3, 16, 384), BF16),
        pltpu.VMEM((48, 384), BF16),
        pltpu.VMEM((48, 384), BF16),
        pltpu.VMEM((2, 384, 896), F32),
        pltpu.VMEM((896, 384), F32),
        sem((4,)), sem((3,)), sem((3,)),
        sem(()), sem((2, 3)), sem((2,)), sem(()), sem((2,)), sem((2,)), sem((2,)), sem((2, 2)), sem(()), sem((STAGES, 2)),
        sem((2,)), sem((STAGES, 3, 2)), sem((STAGES, 3)), sem((2,)), sem((STAGES, 3)),
        sem((2,)), sem((STAGES, 3, 2)), sem((STAGES, 3)), sem((2,)), sem((STAGES, 3)),
        sem(()), sem((TILES, 2)), sem((2,)), sem((TILES, 2)), sem((3,)),
    ]
    results = pl.pallas_call(
        functools.partial(kernel, scale),
        out_shape=(
            pltpu.VMEM((48, 384), BF16),
            pltpu.VMEM((48, 384), BF16),
            pltpu.VMEM((384, 896), F32),
            pltpu.VMEM((384, 896), F32),
            pltpu.VMEM((896, 384), F32),
        ),
        in_specs=[pl.BlockSpec(memory_space=pltpu.HBM)] * 5,
        out_specs=(hbm,) * 5,
        scratch_shapes=scratch,
        compiler_params=pltpu.CompilerParams(
            collective_id=0, has_side_effects=True, vmem_limit_bytes=36 * 1024 * 1024,
        ),
        cost_estimate=pl.CostEstimate(
            flops=2 * 9 * 768 * 384 * 896, bytes_accessed=8 * 1024 * 1024, transcendentals=0,
        ),
        name="ffn",
    )(*(
        pltpu.with_memory_space_constraint(a, pltpu.HBM)
        for a in (tokens.reshape(TILES, 16, 384), gate_weight, up_weight, down_weight,
                  cotangent.reshape(TILES, 16, 384))
    ))
    return pl.pallas_call(
        write_out,
        out_shape=tuple(jax.ShapeDtypeStruct(r.shape, r.dtype) for r in results),
        in_specs=[vmem] * 5,
        out_specs=(hbm,) * 5,
        scratch_shapes=[sem((5,))],
        compiler_params=pltpu.CompilerParams(vmem_limit_bytes=1024 * 1024),
        name="write_out",
    )(*results)


def solution(mesh):
    return jax.shard_map(
        body,
        mesh=mesh,
        in_specs=(
            P("col", "row"),
            P("row", "col"),
            P("row", "col"),
            P("col", "row"),
            P("col", "row"),
        ),
        out_specs=(
            P("col", "row"),
            P("col", "row"),
            P("row", "col"),
            P("row", "col"),
            P("col", "row"),
        ),
        check_vma=False,
    )
```

time: 79.1 us -> 74.9 us (0.947)
  Pallas kernels: 78.4 us -> 74.2 us
    pallas_call x1, Pallas kernels: 76.4 us -> 72.1 us  [body(): pl.pallas_call(functools.partial(kernel, scale), out_shape=(pltpu.VMEM((4...]
where the time goes in v3:
time: 74.9 us; the launch traced here: 74.8 us
  Pallas kernels  74.2 us (99%)
    pallas_call x1, Pallas kernels, body(): pl.pallas_call(functools.partial(kernel, scale), out_shape=(pltpu.VMEM((4...  72.1 us
    pallas_call x1, Pallas kernels, body(): pl.pallas_call(write_out, out_shape=tuple((jax.ShapeDtypeStruct(r.shape,...  2.06 us

profile of v3, /device:TPU:1, one launch (start us, length us, event | category | flops | bytes accessed | tf_op | source)
XLA Modules:
  0.0 74.8 jit_solution(8901560915748018378)
XLA Ops:
  0.6 72.1 %ffn.1 = (bf16[48,384]{1,0:T(8,128)(2,1)S(1)}, bf16[48,384]{1,0:T(8,128)(2,1)S(1)}, f32[384,896]{1,0:T(8,128)S(1)}, f32[384,896]{1,0:T(8,128)S(1)}, f32[896,384]{1,0:T(8,128)S(1)}) custom-call(bf16[3,16,384]{2,1,0:T(8,128)(2,1)} %bitcast.2, bf16[384,896]{1,0:T(8,128)(2,1)} %wg_in.1, bf16[384,896]{1,0:T(8,128)(2,1)} %wu_in.1, bf16[896,384]{1,0:T(8,128)(2,1)} %wd_in.1, ...), custom_call_target="tpu_custom_call" | custom-call | flops 4756340736 | bytes 8388608 | tf_op jit(solution)/shard_map/ffn/pallas_call | solution.py:430
  72.8 2.1 %write_out.1 = (bf16[48,384]{1,0:T(8,128)(2,1)}, bf16[48,384]{1,0:T(8,128)(2,1)}, f32[384,896]{1,0:T(8,128)}, f32[384,896]{1,0:T(8,128)}, f32[896,384]{1,0:T(8,128)}) custom-call(bf16[48,384]{1,0:T(8,128)(2,1)S(1)} %get-tuple-element.10.refs_0_, bf16[48,384]{1,0:T(8,128)(2,1)S(1)} %get-tuple-element.11.refs_1_, f32[384,896]{1,0:T(8,128)S(1)} %get-tuple-element.12.refs_2_, ...), custom_call_target="tpu_custom_call" | custom-call | tf_op jit(solution)/shard_map/write_out/pallas_call | solution.py:454

commit v4 on v3

--- a/solution.py
+++ b/solution.py
@@ -9,7 +9,7 @@
 
 TILES = 3
 STRAIGHT = (0,)
-WHOLE = (3,)
+WHOLE = (0, 3)
 BF16 = jnp.bfloat16
 F32 = jnp.float32
 
@@ -20,9 +20,9 @@
 
 STRIPS = (
     ((0, 0), (0, 1)),
-    ((1, 0), (1, 1), (3, 0), (3, 1)),
-    ((0, 2), (1, 2), (3, 2), (2, 0)),
-    ((2, 1), (2, 2)),
+    ((1, 0), (3, 0), (2, 0), (0, 2)),
+    ((1, 1), (3, 1), (2, 1), (2, 2)),
+    ((1, 2), (3, 2)),
 )
 STAGES = len(STRIPS)
 SMALL = (0, 3)
@@ -31,15 +31,14 @@
 def kernel(
     scale,
     tok_in, wg_in, wu_in, wd_in, cot_in,
-    out_any, gin_any, gg_any, gu_any, gd_any,
+    out_ref, gin_ref, gg, gu, gd,
     panel, other, wg, wu, wd,
     part_s, part_l, own_s, own_l, pairs_s, pairs_l, rs_x_s, rs_x_l, zs_s, zs_l, zr_s, zr_l, hid_s, hid_l,
     oparts, oparts_own, rs_y, zout, zout_b, rs_z, rs_z_b,
-    out_ref, gin_ref, big, gd,
     load_sem, wsend, wrecv,
     azs, azr, azr_b, ats, atr, ays, ayr, ayr_b, afs, afr,
     xrs, xpr, xrr, z4s, z4r, xas, xar, xbr, hfs, hfr,
-    yrs, yrr, zrs, zrr, store_sem,
+    yrs, yrr, zrs, zrr,
 ):
     row = lax.axis_index("row")
     col = lax.axis_index("col")
@@ -71,7 +70,6 @@
     zs = [pick(s, zs_s, zs_l) for s in range(STAGES)]
     zr = [pick(s, zr_s, zr_l) for s in range(STAGES)]
     hid = [pick(s, hid_s, hid_l) for s in range(STAGES)]
-    gg, gu = big.at[0], big.at[1]
 
     def settle(sem, ref):
         pltpu.make_async_copy(ref, ref, sem).wait()
@@ -115,9 +113,9 @@
             )
 
     def send_near(tc, t):
-        src = tiles(first, tc, t) if t else ins[tc].at[first]
-        for d in (1, 3):
-            remote(src, tiles(first, tc, t), ats, atr.at[tc], at(dy=d))
+        src = tiles(0, tc, t) if t else ins[tc].at[0]
+        for d in (1, 3, 2):
+            remote(src, tiles(0, tc, t), ats, atr.at[tc], at(dy=d))
 
     wx = []
 
@@ -133,28 +131,26 @@
             settle(azr.at[tc, t - 1], tiles(first, tc, t))
             send_near(tc, t)
 
-    def gather_last(tc):
+    def take_last(tc):
         settle(azr_b.at[tc], other.at[0, tc, pl.ds(0, 3), 0])
+
+    def gather_mid(tc):
+        for d, js in ((1, pl.ds(1, 1)), (3, pl.ds(1, 1)), (2, pl.ds(1, 2))):
+            block = panel.at[js, tc, :, y]
+            remote(block, block, ays.at[0], ayr.at[tc], at(dy=d))
+
+    def gather_end(tc):
         block = panel.at[last, tc, :, y]
         for d in (1, 3):
-            remote(block, block, ays.at[0], ayr_b.at[tc, 0], at(dy=d))
-
-    def gather_far(tc):
-        block = panel.at[pl.ds(0, 1), tc, :, y]
-        remote(block, block, ays.at[0], ayr.at[tc], at(dy=2))
-
-    def gather_end(tc):
-        block = panel.at[pl.ds(1, 2), tc, :, y]
-        remote(block, block, ays.at[1], ayr_b.at[tc, 1], at(dy=2))
+            remote(block, block, ays.at[1], ayr_b.at[tc], at(dy=d))
 
     def forward_core(s, tc):
         if s == 1:
-            settle(atr.at[tc], other.at[0])
+            settle(atr.at[tc], other.at[:, :, pl.ds(0, 2), 0])
         if s == 2:
-            settle(ayr_b.at[tc, 0], other.at[0, tc])
-            settle(ayr.at[tc], other.at[0, tc, pl.ds(0, 2)])
+            settle(ayr.at[tc], other.at[0])
         if s == 3:
-            settle(ayr_b.at[tc, 1], other.at[0, tc])
+            settle(ayr_b.at[tc], other.at[0, tc])
         for dy in sorted({dy for dy, _ in STRIPS[s]}):
             js = [j for d, j in STRIPS[s] if d == dy]
             js = pl.ds(js[0], len(js))
@@ -181,34 +177,33 @@
         ssem = xrs.at[kind(s)]
         if s in STRAIGHT:
             if s in SMALL:
-                remote(part[s].at[a, (x + 2) % 4], pairs[s].at[a, 0], ssem, xpr.at[s, a, 0], at(dx=2))
+                remote(part[s].at[a, (x + 2) % 4], pairs[s].at[a, 0], ssem, xpr.at[s, a], at(dx=2))
             else:
                 for i in range(2):
                     remote(part[s].at[a, (x + 2) % 4, pl.ds(16 * i, 16)], pairs[s].at[a, i],
-                           ssem, xpr.at[s, a, i], at(dx=2))
+                           ssem, xpr.at[s, a], at(dx=2))
             for i, d in enumerate((1, 3)):
                 remote(part[s].at[a, (x + d) % 4], rs_x[s].at[a, i], ssem, xrr.at[s, a], at(dx=d))
         elif s in SMALL:
-            remote(part[s].at[a, (x + 2) % 4], pairs[s].at[a, 0], ssem, xpr.at[s, a, 0], at(dx=turn))
+            remote(part[s].at[a, (x + 2) % 4], pairs[s].at[a, 0], ssem, xpr.at[s, a], at(dx=turn))
             remote(part[s].at[a, (x + 4 - turn) % 4], rs_x[s].at[a, 1], ssem, xrr.at[s, a], at(dx=4 - turn))
         else:
             for i, d in enumerate((1, 3)):
                 remote(part[s].at[a, (x + 2) % 4, pl.ds(16 * i, 16)], pairs[s].at[a, i],
-                       ssem, xpr.at[s, a, i], at(dx=d))
+                       ssem, xpr.at[s, a], at(dx=d))
             for i, d in enumerate((1, 3)):
                 rows = pl.ds(16 - 16 * i, 16)
                 remote(part[s].at[a, (x + d) % 4, rows], rs_x[s].at[a, i, rows], ssem, xrr.at[s, a], at(dx=d))
 
     def pass_on(s, a):
         ssem = xrs.at[kind(s)]
+        settle(xpr.at[s, a], pairs[s].at[a])
         if s in SMALL:
-            settle(xpr.at[s, a, 0], pairs[s].at[a, 0])
             both = part_own[s][a, (x + turn) % 4] + pairs[s][a, 0].astype(F32)
             part[s][a, (x + turn) % 4] = both.astype(BF16)
             remote(part[s].at[a, (x + turn) % 4], rs_x[s].at[a, 0], ssem, xrr.at[s, a], at(dx=turn))
             return
         for i, d in enumerate((1, 3)):
-            settle(xpr.at[s, a, i], pairs[s].at[a, i])
             rows = pl.ds(16 * i, 16)
             both = part_own[s][a, (x + d) % 4, rows] + pairs[s][a, i].astype(F32)
             part[s][a, (x + d) % 4, rows] = both.astype(BF16)
@@ -218,12 +213,11 @@
         settle(xrr.at[s, a], rs_x[s].at[a])
         total = part_own[s][a, x] + rs_x[s][a, 0].astype(F32) + rs_x[s][a, 1].astype(F32)
         if s in STRAIGHT:
-            for i in range(1 if s in SMALL else 2):
-                settle(xpr.at[s, a, i], pairs[s].at[a, i])
+            settle(xpr.at[s, a], pairs[s].at[a])
             total = total + pairs[s][a].reshape(total.shape).astype(F32)
         part_own[s][a, x] = total
         zs[s][a] = total.astype(BF16)
-        remote(zs[s].at[a], zr[s].at[a], z4s.at[kind(s)], z4r.at[s, a], at(dz4=1))
+        remote(zs[s].at[a], zr[s].at[a], z4s.at[kind(s)], z4r.at[s, a // 2], at(dz4=1))
 
     def spread(s, a, value):
         hid[s][a, k, x] = value.astype(BF16)
@@ -231,19 +225,18 @@
         if s in WHOLE:
             remote(piece, piece, xas.at[kind(s)], xbr.at[s, a], at(dx=2))
         for d in (1, 3):
-            remote(piece, piece, xas.at[kind(s)], xar.at[s, a, d // 2], at(dx=d))
+            remote(piece, piece, xas.at[kind(s)], xar.at[s, a], at(dx=d))
 
     def gate_up(s):
         return tuple(part_own[s][a, x] + zr[s][a].astype(F32) for a in range(2))
 
     def forward(s):
-        settle(z4r.at[s, 0], zr[s].at[0])
-        settle(z4r.at[s, 1], zr[s].at[1])
+        settle(z4r.at[s, 0], zr[s].at[pl.ds(0, 2)])
         gate, up = gate_up(s)
         spread(s, 0, gate * jax.nn.sigmoid(gate) * up)
 
     def backward(s):
-        settle(z4r.at[s, 2], zr[s].at[2])
+        settle(z4r.at[s, 1], zr[s].at[2])
         gate, up = gate_up(s)
         sig = jax.nn.sigmoid(gate)
         d_hidden = part_own[s][2, x] + zr[s][2].astype(F32)
@@ -251,21 +244,18 @@
         spread(s, 2, d_hidden * gate * sig)
 
     def relay(s, a):
+        settle(xar.at[s, a], hid[s].at[a, k, pl.ds(0, 2)])
         if s in SMALL:
-            for i, d in enumerate((1, 3)):
-                settle(xar.at[s, a, i], hid[s].at[a, k, (x + 4 - d) % 4])
             piece = hid[s].at[a, k, (x + 4 - turn) % 4]
             remote(piece, piece, xas.at[0], xbr.at[s, a], at(dx=turn))
             return
         for i, d in enumerate((1, 3)):
-            settle(xar.at[s, a, i], hid[s].at[a, k, (x + 4 - d) % 4])
             piece = hid[s].at[a, k, (x + 4 - d) % 4, pl.ds(16 * i, 16)]
             remote(piece, piece, xas.at[1], xbr.at[s, a], at(dx=d))
 
     def forward_hidden(s, a):
         if s in WHOLE:
-            for i, d in enumerate((1, 3)):
-                settle(xar.at[s, a, i], hid[s].at[a, k, (x + 4 - d) % 4])
+            settle(xar.at[s, a], hid[s].at[a, k, pl.ds(0, 2)])
         settle(xbr.at[s, a], hid[s].at[a, k, (x + 2) % 4])
         remote(hid[s].at[a, k], hid[s].at[a, k], hfs.at[kind(s)], hfr.at[s, a], at(dk=1))
 
@@ -312,7 +302,7 @@
         acc[...] = term
 
     def sums(j):
-        return (zout_b, rs_z_b, j - 1, zrs.at[1]) if j else (zout, rs_z, 0, zrs.at[0])
+        return (zout_b, rs_z_b, 0, zrs.at[1]) if j == 2 else (zout, rs_z, j, zrs.at[0])
 
     def sum_y(j, b):
         settle(yrr.at[j, b], rs_y.at[j, b])
@@ -333,47 +323,38 @@
             total = total + theirs[i, b, d - 1].astype(F32)
         (out_ref, gin_ref)[b][pl.ds(16 * j, 16)] = total.astype(BF16)
 
-    def store(i):
-        src = (out_ref, gin_ref, gg, gu, gd)[i]
-        dst = (out_any, gin_any, gg_any, gu_any, gd_any)[i]
-        pltpu.make_async_copy(src, dst, store_sem.at[(0, 0, 1, 1, 2)[i]]).start()
-
     steps = (
-        (send_z, 0, 0), (send_near, 1, 0), (send_z, 1, 0), (own_tiles,), (send_near, 0, 0), (send_weights,),
-        (send_z, 0, 1), (gather_near, 0), (forward_core, 0, 0), (gather_last, 0), (send_z, 1, 1), (partial, 0, 0),
-        (gather_near, 1), (forward_core, 0, 1), (partial, 0, 1), (forward_core, 1, 0), (gather_far, 0),
-        (gather_end, 0), (partial, 0, 2), (partial, 1, 0), (partial, 1, 1), (sum_x, 0, 0), (forward_core, 1, 1),
-        (sum_x, 0, 1), (sum_x, 0, 2), (gather_far, 1), (forward_core, 2, 0), (gather_last, 1), (pass_on, 1, 0),
-        (gather_end, 1), (partial, 1, 2), (forward_core, 3, 0), (pass_on, 1, 1), (partial, 2, 0), (partial, 2, 1),
-        (sum_x, 1, 0), (pass_on, 1, 2), (forward_core, 2, 1), (sum_x, 1, 1), (forward, 0), (partial, 3, 0),
-        (pass_on, 2, 0), (pass_on, 2, 1), (partial, 2, 2), (sum_x, 1, 2), (partial, 3, 1), (backward, 0),
-        (forward_core, 3, 1), (sum_x, 2, 0), (pass_on, 2, 2), (sum_x, 2, 1), (relay, 0, 0), (partial, 3, 2),
-        (pass_on, 3, 0), (pass_on, 3, 1), (forward, 1), (relay, 0, 2), (relay, 0, 1), (sum_x, 2, 2), (pass_on, 3, 2),
-        (backward, 1), (sum_x, 3, 0), (relay, 1, 0), (forward_hidden, 0, 0), (forward_hidden, 0, 1),
-        (forward_hidden, 0, 2), (sum_x, 3, 1), (project, 0, 1, 0), (sum_x, 3, 2), (relay, 1, 1), (relay, 1, 2),
-        (forward, 2), (forward_hidden, 1, 0), (backward, 2), (take, 0, 1), (forward_hidden, 1, 1), (take, 1, 0),
-        (take, 0, 2), (forward_hidden, 1, 2), (project, 1, 1, 0), (project, 1, 0, 1), (relay, 2, 0), (forward, 3),
-        (project, 1, 0, 0), (backward, 3), (grads, 0, 0), (take, 1, 1), (take, 1, 2), (project, 1, 1, 1),
-        (relay, 2, 1), (relay, 2, 2), (forward_hidden, 2, 0), (project, 2, 0, 0), (forward_hidden, 3, 0),
-        (project, 3, 0, 0), (take, 0, 0), (project, 0, 1, 1), (take, 2, 0), (project, 2, 0, 1), (project, 0, 0, 1),
-        (grads, 0, 2), (take, 3, 0), (project, 3, 0, 1), (forward_hidden, 3, 1), (forward_hidden, 3, 2),
-        (project, 3, 1, 0), (forward_hidden, 2, 1), (forward_hidden, 2, 2), (project, 2, 1, 0), (project, 0, 0, 0),
-        (take, 3, 2), (take, 3, 1), (project, 3, 1, 1), (take, 2, 1), (grads, 1, 2), (take, 2, 2), (sum_y, 0, 0),
-        (project, 2, 1, 1), (grads, 0, 1), (grads, 1, 1), (grads, 2, 1), (sum_y, 1, 0), (sum_y, 2, 0), (grads, 3, 1),
-        (grads, 2, 2), (sum_y, 1, 1), (sum_y, 2, 1), (store, 3), (grads, 3, 2), (sum_y, 0, 1), (grads, 1, 0),
-        (finish, 2, 0), (finish, 2, 1), (grads, 2, 0), (finish, 1, 1), (grads, 3, 0), (finish, 1, 0), (finish, 0, 0),
-        (store, 2), (store, 4), (store, 0), (finish, 0, 1), (store, 1),
+        (send_z, 0, 0), (send_near, 0, 0), (send_z, 0, 1), (own_tiles,), (send_z, 1, 0), (send_near, 1, 0),
+        (send_weights,), (gather_near, 0), (forward_core, 0, 0), (gather_near, 1), (partial, 0, 0), (send_z, 1, 1),
+        (forward_core, 0, 1), (partial, 0, 1), (take_last, 0), (gather_mid, 0), (partial, 0, 2), (forward_core, 1, 0),
+        (gather_end, 0), (take_last, 1), (partial, 1, 0), (sum_x, 0, 1), (forward_core, 1, 1), (partial, 1, 1),
+        (gather_mid, 1), (sum_x, 0, 2), (forward_core, 2, 0), (sum_x, 0, 0), (pass_on, 1, 0), (partial, 1, 2),
+        (pass_on, 1, 1), (partial, 2, 0), (gather_end, 1), (partial, 2, 1), (forward_core, 3, 0), (sum_x, 1, 0),
+        (forward_core, 2, 1), (pass_on, 1, 2), (partial, 3, 0), (sum_x, 1, 1), (pass_on, 2, 0), (partial, 3, 1),
+        (partial, 2, 2), (forward, 0), (sum_x, 1, 2), (pass_on, 2, 1), (pass_on, 3, 1), (sum_x, 2, 0),
+        (forward_core, 3, 1), (pass_on, 3, 0), (pass_on, 2, 2), (backward, 0), (sum_x, 2, 1), (forward_hidden, 0, 0),
+        (forward, 1), (partial, 3, 2), (sum_x, 2, 2), (backward, 1), (project, 0, 0, 0), (relay, 1, 0),
+        (forward_hidden, 0, 2), (sum_x, 3, 0), (pass_on, 3, 2), (forward_hidden, 0, 1), (sum_x, 3, 1), (take, 0, 2),
+        (relay, 1, 1), (forward, 2), (relay, 1, 2), (take, 0, 0), (project, 0, 1, 0), (forward_hidden, 1, 0),
+        (sum_x, 3, 2), (grads, 0, 2), (backward, 2), (forward_hidden, 1, 1), (project, 1, 0, 0), (take, 1, 0),
+        (relay, 2, 0), (project, 1, 0, 1), (forward_hidden, 1, 2), (forward, 3), (project, 1, 1, 0),
+        (project, 0, 0, 1), (relay, 2, 1), (take, 1, 2), (take, 1, 1), (project, 1, 1, 1), (relay, 2, 2),
+        (backward, 3), (forward_hidden, 2, 0), (project, 2, 0, 0), (sum_y, 0, 0), (grads, 0, 1), (grads, 1, 2),
+        (forward_hidden, 3, 0), (take, 2, 0), (forward_hidden, 2, 1), (project, 2, 0, 1), (forward_hidden, 2, 2),
+        (take, 0, 1), (project, 2, 1, 0), (grads, 2, 2), (project, 0, 1, 1), (grads, 1, 1), (take, 2, 2),
+        (take, 2, 1), (take, 3, 0), (project, 2, 1, 1), (sum_y, 0, 1), (forward_hidden, 3, 1), (forward_hidden, 3, 2),
+        (project, 3, 0, 0), (grads, 0, 0), (project, 3, 0, 1), (grads, 2, 1), (sum_y, 1, 0), (take, 3, 1),
+        (take, 3, 2), (project, 3, 1, 0), (project, 3, 1, 1), (grads, 3, 2), (grads, 1, 0), (sum_y, 1, 1),
+        (grads, 3, 1), (sum_y, 2, 0), (grads, 2, 0), (sum_y, 2, 1), (grads, 3, 0), (finish, 0, 0), (finish, 0, 1),
+        (finish, 1, 0), (finish, 1, 1), (finish, 2, 0), (finish, 2, 1),
     )
     for step, *where in steps:
         step(*where)
-    settle(store_sem.at[0], other.at[:, :, 0, 0])
-    settle(store_sem.at[1], big)
-    settle(store_sem.at[2], gd)
     for i, ref in enumerate((wg, wu, wd)):
         settle(wsend.at[i], ref.at[1])
     settle(azs, other.at[:, :, pl.ds(0, 3), 0])
-    settle(ats, other.at[pl.ds(0, 2)])
-    settle(ays.at[0], other.at[:, :, :, 0])
+    settle(ats, other.at[:, :, :, 0])
+    settle(ays.at[0], other.at[pl.ds(0, 2)])
     settle(ays.at[1], other.at[0])
     settle(afs, other)
     for i, ref in enumerate((part_s, part_l)):
@@ -413,19 +394,15 @@
         pltpu.VMEM((TILES, 2, 2, 4, 32, 384), BF16),
         pltpu.VMEM((TILES, 2, 2, 4, 32, 384), F32),
         pltpu.VMEM((TILES, 2, 3, 2, 32, 384), BF16),
-        pltpu.VMEM((1, 2, 4, 16, 384), F32),
-        pltpu.VMEM((2, 2, 4, 16, 384), BF16),
-        pltpu.VMEM((1, 2, 3, 16, 384), F32),
-        pltpu.VMEM((2, 2, 3, 16, 384), BF16),
-        pltpu.VMEM((48, 384), BF16),
-        pltpu.VMEM((48, 384), BF16),
-        pltpu.VMEM((2, 384, 896), F32),
-        pltpu.VMEM((896, 384), F32),
+        pltpu.VMEM((2, 2, 4, 16, 384), F32),
+        pltpu.VMEM((1, 2, 4, 16, 384), BF16),
+        pltpu.VMEM((2, 2, 3, 16, 384), F32),
+        pltpu.VMEM((1, 2, 3, 16, 384), BF16),
         sem((4,)), sem((3,)), sem((3,)),
-        sem(()), sem((2, 3)), sem((2,)), sem(()), sem((2,)), sem((2,)), sem((2,)), sem((2, 2)), sem(()), sem((STAGES, 2)),
-        sem((2,)), sem((STAGES, 3, 2)), sem((STAGES, 3)), sem((2,)), sem((STAGES, 3)),
-        sem((2,)), sem((STAGES, 3, 2)), sem((STAGES, 3)), sem((2,)), sem((STAGES, 3)),
-        sem(()), sem((TILES, 2)), sem((2,)), sem((TILES, 2)), sem((3,)),
+        sem(()), sem((2, 3)), sem((2,)), sem(()), sem((2,)), sem((2,)), sem((2,)), sem((2,)), sem(()), sem((STAGES, 2)),
+        sem((2,)), sem((STAGES, 3)), sem((STAGES, 3)), sem((2,)), sem((STAGES, 2)),
+        sem((2,)), sem((STAGES, 3)), sem((STAGES, 3)), sem((2,)), sem((STAGES, 3)),
+        sem(()), sem((TILES, 2)), sem((2,)), sem((TILES, 2)),
     ]
     results = pl.pallas_call(
         functools.partial(kernel, scale),
@@ -437,7 +414,7 @@
             pltpu.VMEM((896, 384), F32),
         ),
         in_specs=[pl.BlockSpec(memory_space=pltpu.HBM)] * 5,
-        out_specs=(hbm,) * 5,
+        out_specs=(vmem,) * 5,
         scratch_shapes=scratch,
         compiler_params=pltpu.CompilerParams(
             collective_id=0, has_side_effects=True, vmem_limit_bytes=36 * 1024 * 1024,

time: 74.9 us -> 74.5 us (level)
  no operation moved by 1% of the time
where the time goes in v4:
time: 74.5 us; the launch traced here: 74.4 us
  Pallas kernels  73.8 us (99%)
    pallas_call x1, Pallas kernels, body(): pl.pallas_call(functools.partial(kernel, scale), out_shape=(pltpu.VMEM((4...  71.8 us
    pallas_call x1, Pallas kernels, body(): pl.pallas_call(write_out, out_shape=tuple((jax.ShapeDtypeStruct(r.shape,...  2.06 us

profile of v4, /device:TPU:1, one launch (start us, length us, event | category | flops | bytes accessed | tf_op | source)
XLA Modules:
  0.0 74.4 jit_solution(14749289546433829426)
XLA Ops:
  0.6 71.8 %ffn.1 = (bf16[48,384]{1,0:T(8,128)(2,1)S(1)}, bf16[48,384]{1,0:T(8,128)(2,1)S(1)}, f32[384,896]{1,0:T(8,128)S(1)}, f32[384,896]{1,0:T(8,128)S(1)}, f32[896,384]{1,0:T(8,128)S(1)}) custom-call(bf16[3,16,384]{2,1,0:T(8,128)(2,1)} %bitcast.2, bf16[384,896]{1,0:T(8,128)(2,1)} %wg_in.1, bf16[384,896]{1,0:T(8,128)(2,1)} %wu_in.1, bf16[896,384]{1,0:T(8,128)(2,1)} %wd_in.1, ...), custom_call_target="tpu_custom_call" | custom-call | flops 4756340736 | bytes 8388608 | tf_op jit(solution)/shard_map/ffn/pallas_call | solution.py:407
  72.4 2.1 %write_out.1 = (bf16[48,384]{1,0:T(8,128)(2,1)}, bf16[48,384]{1,0:T(8,128)(2,1)}, f32[384,896]{1,0:T(8,128)}, f32[384,896]{1,0:T(8,128)}, f32[896,384]{1,0:T(8,128)}) custom-call(bf16[48,384]{1,0:T(8,128)(2,1)S(1)} %get-tuple-element.10.refs_0_, bf16[48,384]{1,0:T(8,128)(2,1)S(1)} %get-tuple-element.11.refs_1_, f32[384,896]{1,0:T(8,128)S(1)} %get-tuple-element.12.refs_2_, ...), custom_call_target="tpu_custom_call" | custom-call | tf_op jit(solution)/shard_map/write_out/pallas_call | solution.py:431

commit v5 on v4

--- a/solution.py
+++ b/solution.py
@@ -336,17 +336,17 @@
         (forward, 1), (partial, 3, 2), (sum_x, 2, 2), (backward, 1), (project, 0, 0, 0), (relay, 1, 0),
         (forward_hidden, 0, 2), (sum_x, 3, 0), (pass_on, 3, 2), (forward_hidden, 0, 1), (sum_x, 3, 1), (take, 0, 2),
         (relay, 1, 1), (forward, 2), (relay, 1, 2), (take, 0, 0), (project, 0, 1, 0), (forward_hidden, 1, 0),
-        (sum_x, 3, 2), (grads, 0, 2), (backward, 2), (forward_hidden, 1, 1), (project, 1, 0, 0), (take, 1, 0),
-        (relay, 2, 0), (project, 1, 0, 1), (forward_hidden, 1, 2), (forward, 3), (project, 1, 1, 0),
-        (project, 0, 0, 1), (relay, 2, 1), (take, 1, 2), (take, 1, 1), (project, 1, 1, 1), (relay, 2, 2),
-        (backward, 3), (forward_hidden, 2, 0), (project, 2, 0, 0), (sum_y, 0, 0), (grads, 0, 1), (grads, 1, 2),
-        (forward_hidden, 3, 0), (take, 2, 0), (forward_hidden, 2, 1), (project, 2, 0, 1), (forward_hidden, 2, 2),
-        (take, 0, 1), (project, 2, 1, 0), (grads, 2, 2), (project, 0, 1, 1), (grads, 1, 1), (take, 2, 2),
-        (take, 2, 1), (take, 3, 0), (project, 2, 1, 1), (sum_y, 0, 1), (forward_hidden, 3, 1), (forward_hidden, 3, 2),
-        (project, 3, 0, 0), (grads, 0, 0), (project, 3, 0, 1), (grads, 2, 1), (sum_y, 1, 0), (take, 3, 1),
-        (take, 3, 2), (project, 3, 1, 0), (project, 3, 1, 1), (grads, 3, 2), (grads, 1, 0), (sum_y, 1, 1),
-        (grads, 3, 1), (sum_y, 2, 0), (grads, 2, 0), (sum_y, 2, 1), (grads, 3, 0), (finish, 0, 0), (finish, 0, 1),
-        (finish, 1, 0), (finish, 1, 1), (finish, 2, 0), (finish, 2, 1),
+        (sum_x, 3, 2), (grads, 0, 2), (backward, 2), (take, 0, 1), (project, 0, 1, 1), (forward_hidden, 1, 1),
+        (project, 1, 0, 0), (take, 1, 0), (relay, 2, 0), (project, 1, 0, 1), (forward_hidden, 1, 2), (forward, 3),
+        (project, 1, 1, 0), (project, 0, 0, 1), (relay, 2, 1), (take, 1, 2), (take, 1, 1), (project, 1, 1, 1),
+        (relay, 2, 2), (backward, 3), (forward_hidden, 2, 0), (project, 2, 0, 0), (sum_y, 0, 0), (grads, 0, 1),
+        (grads, 1, 2), (forward_hidden, 3, 0), (take, 2, 0), (forward_hidden, 2, 1), (project, 2, 0, 1),
+        (forward_hidden, 2, 2), (project, 2, 1, 0), (take, 2, 2), (take, 2, 1), (take, 3, 0), (project, 2, 1, 1),
+        (sum_y, 0, 1), (forward_hidden, 3, 1), (forward_hidden, 3, 2), (project, 3, 0, 0), (project, 3, 0, 1),
+        (sum_y, 1, 0), (take, 3, 1), (take, 3, 2), (project, 3, 1, 0), (project, 3, 1, 1), (grads, 0, 0),
+        (grads, 1, 0), (grads, 1, 1), (sum_y, 1, 1), (grads, 2, 0), (grads, 2, 1), (sum_y, 2, 0), (grads, 2, 2),
+        (sum_y, 2, 1), (grads, 3, 0), (grads, 3, 1), (grads, 3, 2), (finish, 0, 0), (finish, 0, 1), (finish, 1, 0),
+        (finish, 1, 1), (finish, 2, 0), (finish, 2, 1),
     )
     for step, *where in steps:
         step(*where)

time: 74.5 us -> 74.6 us (level)
  no operation moved by 1% of the time
where the time goes in v5:
time: 74.6 us; the launch traced here: 74.5 us
  Pallas kernels  73.8 us (99%)
    pallas_call x1, Pallas kernels, body(): pl.pallas_call(functools.partial(kernel, scale), out_shape=(pltpu.VMEM((4...  71.8 us
    pallas_call x1, Pallas kernels, body(): pl.pallas_call(write_out, out_shape=tuple((jax.ShapeDtypeStruct(r.shape,...  2.06 us

profile of v5, /device:TPU:1, one launch (start us, length us, event | category | flops | bytes accessed | tf_op | source)
XLA Modules:
  0.0 74.5 jit_solution(1399094082049810337)
XLA Ops:
  0.6 71.8 %ffn.1 = (bf16[48,384]{1,0:T(8,128)(2,1)S(1)}, bf16[48,384]{1,0:T(8,128)(2,1)S(1)}, f32[384,896]{1,0:T(8,128)S(1)}, f32[384,896]{1,0:T(8,128)S(1)}, f32[896,384]{1,0:T(8,128)S(1)}) custom-call(bf16[3,16,384]{2,1,0:T(8,128)(2,1)} %bitcast.2, bf16[384,896]{1,0:T(8,128)(2,1)} %wg_in.1, bf16[384,896]{1,0:T(8,128)(2,1)} %wu_in.1, bf16[896,384]{1,0:T(8,128)(2,1)} %wd_in.1, ...), custom_call_target="tpu_custom_call" | custom-call | flops 4756340736 | bytes 8388608 | tf_op jit(solution)/shard_map/ffn/pallas_call | solution.py:407
  72.4 2.1 %write_out.1 = (bf16[48,384]{1,0:T(8,128)(2,1)}, bf16[48,384]{1,0:T(8,128)(2,1)}, f32[384,896]{1,0:T(8,128)}, f32[384,896]{1,0:T(8,128)}, f32[896,384]{1,0:T(8,128)}) custom-call(bf16[48,384]{1,0:T(8,128)(2,1)S(1)} %get-tuple-element.10.refs_0_, bf16[48,384]{1,0:T(8,128)(2,1)S(1)} %get-tuple-element.11.refs_1_, f32[384,896]{1,0:T(8,128)S(1)} %get-tuple-element.12.refs_2_, ...), custom_call_target="tpu_custom_call" | custom-call | tf_op jit(solution)/shard_map/write_out/pallas_call | solution.py:431

commit v6 on v4

--- a/solution.py
+++ b/solution.py
@@ -342,7 +342,7 @@
         (backward, 3), (forward_hidden, 2, 0), (project, 2, 0, 0), (sum_y, 0, 0), (grads, 0, 1), (grads, 1, 2),
         (forward_hidden, 3, 0), (take, 2, 0), (forward_hidden, 2, 1), (project, 2, 0, 1), (forward_hidden, 2, 2),
         (take, 0, 1), (project, 2, 1, 0), (grads, 2, 2), (project, 0, 1, 1), (grads, 1, 1), (take, 2, 2),
-        (take, 2, 1), (take, 3, 0), (project, 2, 1, 1), (sum_y, 0, 1), (forward_hidden, 3, 1), (forward_hidden, 3, 2),
+        (take, 2, 1), (take, 3, 0), (forward_hidden, 3, 1), (forward_hidden, 3, 2), (project, 2, 1, 1), (sum_y, 0, 1),
         (project, 3, 0, 0), (grads, 0, 0), (project, 3, 0, 1), (grads, 2, 1), (sum_y, 1, 0), (take, 3, 1),
         (take, 3, 2), (project, 3, 1, 0), (project, 3, 1, 1), (grads, 3, 2), (grads, 1, 0), (sum_y, 1, 1),
         (grads, 3, 1), (sum_y, 2, 0), (grads, 2, 0), (sum_y, 2, 1), (grads, 3, 0), (finish, 0, 0), (finish, 0, 1),

time: 74.5 us -> 73.9 us (level)
  no operation moved by 1% of the time
where the time goes in v6:
time: 73.9 us; the launch traced here: 73.8 us
  Pallas kernels  73.2 us (99%)
    pallas_call x1, Pallas kernels, body(): pl.pallas_call(functools.partial(kernel, scale), out_shape=(pltpu.VMEM((4...  71.1 us
    pallas_call x1, Pallas kernels, body(): pl.pallas_call(write_out, out_shape=tuple((jax.ShapeDtypeStruct(r.shape,...  2.06 us

profile of v6, /device:TPU:1, one launch (start us, length us, event | category | flops | bytes accessed | tf_op | source)
XLA Modules:
  0.0 73.8 jit_solution(1718190744634147928)
XLA Ops:
  0.6 71.1 %ffn.1 = (bf16[48,384]{1,0:T(8,128)(2,1)S(1)}, bf16[48,384]{1,0:T(8,128)(2,1)S(1)}, f32[384,896]{1,0:T(8,128)S(1)}, f32[384,896]{1,0:T(8,128)S(1)}, f32[896,384]{1,0:T(8,128)S(1)}) custom-call(bf16[3,16,384]{2,1,0:T(8,128)(2,1)} %bitcast.2, bf16[384,896]{1,0:T(8,128)(2,1)} %wg_in.1, bf16[384,896]{1,0:T(8,128)(2,1)} %wu_in.1, bf16[896,384]{1,0:T(8,128)(2,1)} %wd_in.1, ...), custom_call_target="tpu_custom_call" | custom-call | flops 4756340736 | bytes 8388608 | tf_op jit(solution)/shard_map/ffn/pallas_call | solution.py:407
  71.8 2.1 %write_out.1 = (bf16[48,384]{1,0:T(8,128)(2,1)}, bf16[48,384]{1,0:T(8,128)(2,1)}, f32[384,896]{1,0:T(8,128)}, f32[384,896]{1,0:T(8,128)}, f32[896,384]{1,0:T(8,128)}) custom-call(bf16[48,384]{1,0:T(8,128)(2,1)S(1)} %get-tuple-element.10.refs_0_, bf16[48,384]{1,0:T(8,128)(2,1)S(1)} %get-tuple-element.11.refs_1_, f32[384,896]{1,0:T(8,128)S(1)} %get-tuple-element.12.refs_2_, ...), custom_call_target="tpu_custom_call" | custom-call | tf_op jit(solution)/shard_map/write_out/pallas_call | solution.py:431
